TPU v7x, 32 devices: a whole 2x2x4 slice. The times are simulated.
32 devices in a mesh: seq: 8 (over z, x), head: 4 (over y, core).
Axes of the slice: x: 2, y: 2, z: 4, core: 2. Of those that a mesh axis runs over, the one named last changes fastest.
Arguments:
- inputs: bfloat16 [8192, 8192], P('seq', 'head'), may hold values from -6 to 6
- in_map: bfloat16 [8192, 128], P('seq'), may hold values from -1.25 to 1.25
- out_map: bfloat16 [8192, 128], P('seq'), may hold values from -1.25 to 1.25
- log_decay: float32 [64, 8192], P('head', 'seq'), may hold values from -0.8 to 0, as said below
- cotangent: bfloat16 [8192, 8192], P('seq', 'head'), may hold values from -0.4375 to 0.4375
Outputs:
- grad_inputs: float32 [8192, 8192], P('seq', 'head')
- grad_in_map: float32 [8192, 128], P(('seq', 'head'))
- grad_out_map: float32 [8192, 128], P(('seq', 'head'))
- grad_decay: float32 [64, 8192], P('head', 'seq')
Inputs may be any that keep to these rules, and one draw needn't show every extreme that they name: `log_decay`: entries are negative.
All inputs are finite; a program needn't handle non-finite values.
Results may differ from a plain program's by a relative error of at most 0.00035.
Values sent between devices are 32-bit elements; how exact they have to be, the bound alone decides.
A program may use at most 128 MiB of HBM per device.

v0:
```python
import jax
import jax.numpy as jnp
from jax import lax
from jax.sharding import PartitionSpec as P

BLOCK = 512


highest = lax.Precision.HIGHEST


def prefix(array, axis, combine, identity, reverse):
    peers, mine = (lax.axis_size(axis), lax.axis_index(axis))
    everything = jax.tree.map(lambda part: lax.all_gather(part, axis), array)
    start = jax.tree.map(
        lambda part, zero: jnp.broadcast_to(jnp.asarray(zero, part.dtype), part.shape),
        array,
        identity,
    )

    def hop(k, before):
        at = peers - 1 - k if reverse else k
        reached = at > mine if reverse else at < mine
        new = combine(before, jax.tree.map(lambda part: part[at], everything))
        return jax.tree.map(lambda a, b: jnp.where(reached, a, b), new, before)

    return lax.fori_loop(0, peers, hop, start)


def triangles(length):
    locations = jnp.arange(length)
    upper = (locations[:, None] <= locations[None, :]).astype(jnp.float32)
    return (upper, upper.T)


def local_block(pieces):
    inputs_blk, in_blk, out_blk, rates, cotan_blk = pieces
    upper, lower = triangles(rates.shape[1])
    running = jnp.dot(rates, upper, precision=highest)
    causal = lower[None] > 0
    gaps = running[:, :, None] - running[:, None, :]
    decays = jnp.where(causal, jnp.exp(jnp.where(causal, gaps, 0.0)), 0.0)
    scores = jnp.dot(out_blk, in_blk.T, preferred_element_type=jnp.float32)
    pairs = jnp.einsum("uhp,shp->hus", cotan_blk, inputs_blk, preferred_element_type=jnp.float32)
    weights = decays * scores[None]
    joint = decays * pairs
    cotan_wide = cotan_blk.astype(jnp.float32)
    inputs_wide = inputs_blk.astype(jnp.float32)
    in_wide = in_blk.astype(jnp.float32)
    out_wide = out_blk.astype(jnp.float32)
    grad_inner = jnp.einsum("hus,uhp->shp", weights, cotan_wide, precision=highest)
    in_inner = jnp.einsum("hus,un->sn", joint, out_wide, precision=highest)
    out_inner = jnp.einsum("hts,sn->tn", joint, in_wide, precision=highest)
    product = joint * scores[None]
    column_totals = jnp.sum(product, axis=1)
    row_totals = jnp.sum(product, axis=2)
    inner = (
        jnp.dot(column_totals, upper, precision=highest)
        - jnp.dot(row_totals, upper, precision=highest)
        + row_totals
    )
    to_end = jnp.exp(running[:, -1:] - running)
    from_start = jnp.exp(running)
    state_part = jnp.einsum(
        "shp,sn->hpn", inputs_wide * to_end.T[:, :, None], in_wide, precision=highest
    )
    adjoint_part = jnp.einsum(
        "uhp,un->hpn", cotan_wide * from_start.T[:, :, None], out_wide, precision=highest
    )
    return (
        grad_inner,
        in_inner,
        out_inner,
        inner,
        running,
        state_part,
        adjoint_part,
        from_start[:, -1],
    )


def carried_block(pieces):
    inputs_blk, in_blk, out_blk, cotan_blk, running, grad_inner, inner, start_state, end_adjoint = (
        pieces
    )
    upper, lower = triangles(running.shape[1])
    to_end = jnp.exp(running[:, -1:] - running)
    from_start = jnp.exp(running)
    cotan_wide = cotan_blk.astype(jnp.float32)
    inputs_wide = inputs_blk.astype(jnp.float32)
    in_wide = in_blk.astype(jnp.float32)
    out_wide = out_blk.astype(jnp.float32)
    grad_block = (
        grad_inner
        + jnp.einsum("tn,hpn->thp", in_wide, end_adjoint, precision=highest) * to_end.T[:, :, None]
    )
    feed_out = jnp.einsum("thp,hpn->thn", cotan_wide, start_state, precision=highest)
    out_carried = jnp.einsum("ht,thn->tn", from_start, feed_out, precision=highest)
    from_state = from_start * jnp.einsum("thn,tn->ht", feed_out, out_wide, precision=highest)
    feed_in = jnp.einsum("thp,hpn->thn", inputs_wide, end_adjoint, precision=highest)
    in_carried = jnp.einsum("ht,thn->tn", to_end, feed_in, precision=highest)
    from_adjoint = to_end * jnp.einsum("thn,tn->ht", feed_in, in_wide, precision=highest)
    crossing = from_start[:, -1] * jnp.sum(end_adjoint * start_state, axis=(1, 2))
    own_term = jnp.einsum("thp,thp->ht", inputs_wide, grad_block, precision=highest)
    grad_rates = (
        inner
        + jnp.dot(from_state, lower, precision=highest)
        + jnp.dot(from_adjoint, upper, precision=highest)
        + crossing[:, None]
        - own_term
    )
    return (grad_block, in_carried, out_carried, grad_rates)


def combine(earlier, later):
    first_total, first_value = earlier
    second_total, second_value = later
    return (first_total * second_total, second_total[:, None, None] * first_value + second_value)


def carry_step(carry, item):
    value, factor = carry
    part, decay_total = item
    return ((decay_total[:, None, None] * value + part, factor * decay_total), (value, factor))


def on_device(inputs, in_map, out_map, log_decay, cotangent):
    heads_here = log_decay.shape[0]
    row_count = inputs.shape[0]
    head_width = inputs.shape[1] // heads_here
    blocks_here = row_count // BLOCK
    inputs_blocks = inputs.reshape(blocks_here, BLOCK, heads_here, head_width)
    cotan_blocks = cotangent.reshape(blocks_here, BLOCK, heads_here, head_width)
    in_blocks = in_map.reshape(blocks_here, BLOCK, in_map.shape[1])
    out_blocks = out_map.reshape(blocks_here, BLOCK, out_map.shape[1])
    rate_blocks = log_decay.reshape(heads_here, blocks_here, BLOCK).transpose(1, 0, 2)
    grad_inner, in_inner, out_inner, inner, running, state_parts, adjoint_parts, totals = lax.map(
        local_block, (inputs_blocks, in_blocks, out_blocks, rate_blocks, cotan_blocks)
    )
    zeros_state = jnp.zeros(state_parts.shape[1:], jnp.float32)
    ones_heads = jnp.ones((heads_here,), jnp.float32)
    (device_state, device_total), (start_states, before) = lax.scan(
        carry_step, (zeros_state, ones_heads), (state_parts, totals)
    )
    (device_adjoint, unused_total), (end_adjoints, after) = lax.scan(
        carry_step, (zeros_state, ones_heads), (adjoint_parts, totals), reverse=True
    )
    forward_pair = prefix(
        (device_total, device_state), "seq", combine, (ones_heads, zeros_state), False
    )
    backward_pair = prefix(
        (device_total, device_adjoint), "seq", combine, (ones_heads, zeros_state), True
    )
    state_in = forward_pair[1]
    adjoint_in = backward_pair[1]
    start_states = start_states + before[:, :, None, None] * state_in[None]
    end_adjoints = end_adjoints + after[:, :, None, None] * adjoint_in[None]
    grad_block, in_carried, out_carried, grad_rates = lax.map(
        carried_block,
        (
            inputs_blocks,
            in_blocks,
            out_blocks,
            cotan_blocks,
            running,
            grad_inner,
            inner,
            start_states,
            end_adjoints,
        ),
    )
    grad_inputs = grad_block.reshape(row_count, heads_here * head_width)
    grad_decay = grad_rates.transpose(1, 0, 2).reshape(heads_here, row_count)
    grad_in_map, grad_out_map = (
        lax.psum_scatter(
            (in_inner + in_carried).reshape(row_count, -1), "head", scatter_dimension=0, tiled=True
        ),
        lax.psum_scatter(
            (out_inner + out_carried).reshape(row_count, -1),
            "head",
            scatter_dimension=0,
            tiled=True,
        ),
    )
    return (grad_inputs, grad_in_map, grad_out_map, grad_decay)


def solution(mesh):
    placed = (P("seq", "head"), P("seq", None), P("seq", None), P("head", "seq"), P("seq", "head"))
    return jax.shard_map(
        on_device,
        mesh=mesh,
        in_specs=placed,
        out_specs=(
            P("seq", "head"),
            P(("seq", "head"), None),
            P(("seq", "head"), None),
            P("head", "seq"),
        ),
        check_vma=False,
    )
```

profile of v0, /device:TPU:0, one launch (start us, length us, event | category | flops | bytes accessed | tf_op | source)
XLA Modules:
  0.0 596.4 jit_solution(15510158985178671894)
XLA Ops:
  7.2 5.6 copy.82
  12.9 5.6 copy.83
  21.5 1.6 broadcast.50.clone
  23.0 1.5 broadcast.50.clone.1
  24.6 110.0 %while.108 = (s32[]{:T(128)}, f32[2,512,16,128]{1,3,2,0:T(8,128)}, f32[2,512,128]{2,1,0:T(8,128)}, f32[2,512,128]{2,1,0:T(8,128)}, f32[2,16,512]{2,1,0:T(8,128)}...) while((s32[]{:T(128)}, f32[2,512,16,128]{1,3,2,0:T(8,128)}, ...), condition=%wide.region_4.5_spmd, body=%wide.region_0.4_spmd.sunk | while | flops 11816673280 | bytes 64689976 | solution.py:137
  24.8 2.3 fusion.168
  28.8 5.0 constant_dynamic-slice_fusion.16
  33.8 3.0 copy.124
  36.8 13.7 %bitcast_dynamic-update-slice_fusion.12 = f32[2,512,16,128]{1,3,2,0:T(8,128)} fusion(f32[2,512,16,128]{1,3,2,0:T(8,128)} %get-tuple-element.1269, s32[]{:T(128)S(6)} %copy.162, f32[512,512]{1,0:T(8,128)} %fusion.168, f32[16,512]{1,0:T(8,128)S(1)} %get-tuple-element.1190, pred[512,512]{1,0:T(8,128)(4,1)} %convert_compare_fusion.2, ...), kind=kOutput, calls=%fused_computation.77.clone.1 | convolution fusion | flops 6459228160 | bytes 7667716 | tf_op jit(solution)/shard_map/while/body/eval_jaxpr/hus,uhp->shp/dot_general | solution.py:51
  50.5 10.5 %multiply_reduce_fusion.3 = (f32[16,512]{1,0:T(8,128)S(1)}, f32[16,512]{1,0:T(8,128)S(1)}, f32[512,512]{1,0:T(8,128)S(1)}) fusion(f32[512,512]{1,0:T(8,128)S(1)} %copy-done.12, bf16[1,512,16,128]{3,2,1,0:T(8,128)(2,1)S(1)} %copy-done.2, bf16[1,512,16,128]{1,3,2,0:T(8,128)(2,1)S(1)} %copy.124, f32[16,512]{1,0:T(8,128)S(1)} %get-tuple-element.1190, ...), kind=kOutput, calls=%fused_computation.71.clone.1 | convolution fusion | flops 1107017728 | bytes 6651904 | tf_op jit(solution)/shard_map/while/body/eval_jaxpr/uhp,shp->hus/dot_general | solution.py:44
  61.0 1.9 fusion.169
  65.8 4.3 copy.125
  70.4 4.8 fusion.174
  75.2 4.1 fusion.175
  79.6 2.2 fusion.168
  83.5 5.0 constant_dynamic-slice_fusion.16
  88.5 3.0 copy.124
  91.5 13.7 %bitcast_dynamic-update-slice_fusion.12 = f32[2,512,16,128]{1,3,2,0:T(8,128)} fusion(f32[2,512,16,128]{1,3,2,0:T(8,128)} %get-tuple-element.1269, s32[]{:T(128)S(6)} %copy.162, f32[512,512]{1,0:T(8,128)} %fusion.168, f32[16,512]{1,0:T(8,128)S(1)} %get-tuple-element.1190, pred[512,512]{1,0:T(8,128)(4,1)} %convert_compare_fusion.2, ...), kind=kOutput, calls=%fused_computation.77.clone.1 | convolution fusion | flops 6459228160 | bytes 7667716 | tf_op jit(solution)/shard_map/while/body/eval_jaxpr/hus,uhp->shp/dot_general | solution.py:51
  105.2 10.5 %multiply_reduce_fusion.3 = (f32[16,512]{1,0:T(8,128)S(1)}, f32[16,512]{1,0:T(8,128)S(1)}, f32[512,512]{1,0:T(8,128)S(1)}) fusion(f32[512,512]{1,0:T(8,128)S(1)} %copy-done.12, bf16[1,512,16,128]{3,2,1,0:T(8,128)(2,1)S(1)} %copy-done.2, bf16[1,512,16,128]{1,3,2,0:T(8,128)(2,1)S(1)} %copy.124, f32[16,512]{1,0:T(8,128)S(1)} %get-tuple-element.1190, ...), kind=kOutput, calls=%fused_computation.71.clone.1 | convolution fusion | flops 1107017728 | bytes 6651904 | tf_op jit(solution)/shard_map/while/body/eval_jaxpr/uhp,shp->hus/dot_general | solution.py:44
  115.7 1.9 fusion.169
  120.5 4.3 copy.125
  125.1 4.8 fusion.174
  129.9 4.1 fusion.175
  134.9 3.2 while.111
  139.9 3.2 while.110
  146.4 23.7 %all-reduce = f32[128]{0:T(128)S(1)} all-reduce(f32[128]{0:T(128)S(1)} %dynamic-update-slice), channel_id=2, replica_groups=mesh['seq'=8,'head'=4] {'seq'}, use_global_device_ids=true, to_apply=%add | all-reduce | flops 128 | bytes 1024
  170.2 97.2 %all-gather.8.cloned.1.call-done = f32[128,128,128]{2,1,0:T(8,128)} async-done(((f32[16,128,128]{2,1,0:T(8,128)}), f32[128,128,128]{2,1,0:T(8,128)}) %all-gather.8.cloned.1.call-update) | async-done | bytes 8388624 | tf_op jit(solution)/shard_map/all_gather | solution.py:14
  267.3 12.1 %while.113 = (s32[]{:T(128)}, f32[16,128,128]{2,1,0:T(8,128)S(1)}, s32[]{:T(128)}, f32[8,16]{1,0:T(8,128)S(1)}, f32[8,16,128,128]{3,2,1,0:T(8,128)}, /*index=5*/s32[]{:T(128)}, s32[]{:T(128)}) while((s32[]{:T(128)}, f32[16,128,128]{2,1,0:T(8,128)S(1)}, s32[]{:T(128)}, f32[8,16]{1,0:T(8,128)S(1)}, f32[8,16,128,128]{3,2,1,0:T(8,128)}, ...), condition=%wide.region_8.9_spmd.clone, body=%wide.region_7.8_spmd.clone.sunk | while | flops 1048580 | bytes 3146033 | solution.py:27
  274.8 1.6 fusion.200
  279.5 113.1 %all-gather.6.cloned.1.call-done = f32[128,128,128]{2,1,0:T(8,128)} async-done(((f32[16,128,128]{2,1,0:T(8,128)}), f32[128,128,128]{2,1,0:T(8,128)}) %all-gather.6.cloned.1.call-update) | async-done | bytes 8388624 | tf_op jit(solution)/shard_map/all_gather | solution.py:14
  392.6 12.0 %while.112 = (s32[]{:T(128)}, f32[16,128,128]{2,1,0:T(8,128)S(1)}, s32[]{:T(128)}, f32[8,16]{1,0:T(8,128)S(1)}, f32[8,16,128,128]{3,2,1,0:T(8,128)}, /*index=5*/s32[]{:T(128)}, s32[]{:T(128)}, s32[]{:T(128)}, s32[]{:T(128)}) while((s32[]{:T(128)}, f32[16,128,128]{2,1,0:T(8,128)S(1)}, s32[]{:T(128)}, f32[8,16]{1,0:T(8,128)S(1)}, ...), condition=%wide.region_12.13_spmd.clone, body=%wide.region_11.12_spmd.clone.sunk | while | flops 1048584 | bytes 3146095 | solution.py:27
  404.6 4.6 multiply_add_fusion
  410.9 131.8 %while.109 = (s32[]{:T(128)}, f32[2,512,16,128]{3,2,1,0:T(8,128)}, f32[2,512,128]{2,1,0:T(8,128)}, f32[2,512,128]{2,1,0:T(8,128)}, f32[2,16,512]{2,1,0:T(8,128)S...) while((s32[]{:T(128)}, f32[2,512,16,128]{3,2,1,0:T(8,128)}, ...), condition=%wide.region_15.16_spmd, body=%wide.region_13.15_spmd.sunk | while | flops 4989173760 | bytes 191433168 | solution.py:158
  411.1 2.0 constant_dynamic-slice_fusion.17
  414.2 4.8 constant_dynamic-slice_fusion.19
  418.9 5.3 copy.134
  424.3 5.5 fusion.189
  429.7 4.4 copy_dynamic-update-slice_fusion.2
  435.7 4.4 convolution_bitcast_fusion.6
  440.1 5.5 copy.135
  445.6 5.5 fusion.190
  451.1 4.4 convolution_bitcast_fusion.7
  455.6 5.5 copy.136
  461.0 5.5 fusion.191
  468.0 3.4 fusion.192
  472.7 3.4 fusion.193
  476.8 2.0 constant_dynamic-slice_fusion.17
  479.8 4.8 constant_dynamic-slice_fusion.19
  484.6 5.3 copy.134
  489.9 5.5 fusion.189
  495.4 4.5 copy_dynamic-update-slice_fusion.2
  501.5 4.4 convolution_bitcast_fusion.6
  505.9 5.5 copy.135
  511.3 5.5 fusion.190
  516.9 4.4 convolution_bitcast_fusion.7
  521.3 5.5 copy.136
  526.8 5.5 fusion.191
  533.8 3.4 fusion.192
  538.5 3.4 fusion.193
  542.7 2.1 add.147
  544.9 2.1 add.148
  547.0 11.0 %copy.106 = f32[128,8,16,128]{3,1,2,0:T(8,128)} copy(f32[128,8,16,128]{3,2,1,0:T(8,128)} %bitcast.367) | data formatting | bytes 16777216
  558.7 6.2 %reduce-scatter.3.cloned.1.call-done = f32[256,128]{1,0:T(8,128)} async-done(((f32[1024,128]{1,0:T(8,128)}), f32[256,128]{1,0:T(8,128)}) %reduce-scatter.3.cloned.1.call-update) | async-done | bytes 131088 | tf_op jit(solution)/shard_map/reduce_scatter | solution.py:175
  564.9 24.7 %reduce-scatter.5.cloned.1.call-done = f32[256,128]{1,0:T(8,128)} async-done(((f32[1024,128]{1,0:T(8,128)}), f32[256,128]{1,0:T(8,128)}) %reduce-scatter.5.cloned.1.call-update) | async-done | bytes 131088 | tf_op jit(solution)/shard_map/reduce_scatter | solution.py:178
  (215 shorter events, 60.5 us)
Async XLA Ops:
  7.2 260.2 %all-gather.8.cloned.1.call-start = ((), (), s32[]{:S(2)}) async-start(), calls=%async_computation.5 | async-start | bytes 9437184 | tf_op jit(solution)/shard_map/all_gather | solution.py:14
  7.2 5.6 copy-start.24
  18.5 6.1 %copy-start.11 = (bf16[1024,128]{1,0:T(8,128)(2,1)S(1)}, bf16[1024,128]{1,0:T(8,128)(2,1)}, u32[]{:S(2)}) copy-start(bf16[1024,128]{1,0:T(8,128)(2,1)} %param.18) | copy-start | bytes 786436
  24.6 110.3 %copy-start.6 = (f32[16,128,128]{2,1,0:T(8,128)S(1)}, f32[16,128,128]{2,1,0:T(8,128)}, u32[]{:S(2)}) copy-start(f32[16,128,128]{2,1,0:T(8,128)} %custom-call.2) | copy-start | bytes 3145732
  24.6 110.3 %copy-start.25 = (f32[16]{0:T(128)S(1)}, f32[16]{0:T(128)}, u32[]{:S(2)}) copy-start(f32[16]{0:T(128)} %custom-call.3) | copy-start | bytes 196
  36.8 13.7 %copy-start.2 = (bf16[1,512,16,128]{3,2,1,0:T(8,128)(2,1)S(1)}, bf16[1,512,16,128]{3,2,1,0:T(8,128)(2,1)}, u32[]{:S(2)}) copy-start(bf16[1,512,16,128]{3,2,1,0:T(8,128)(2,1)} %get-tuple-element.1192) | copy-start | bytes 6291460 | tf_op jit(solution)/shard_map/while
  36.8 13.7 %copy-start.12 = (f32[512,512]{1,0:T(8,128)S(1)}, f32[512,512]{1,0:T(8,128)}, u32[]{:S(2)}) copy-start(f32[512,512]{1,0:T(8,128)} %fusion.168) | copy-start | bytes 3145732 | tf_op jit(solution)/shard_map/while
  36.8 13.7 %copy-start.15 = (pred[512,512]{1,0:T(8,128)(4,1)S(1)}, pred[512,512]{1,0:T(8,128)(4,1)}, u32[]{:S(2)}) copy-start(pred[512,512]{1,0:T(8,128)(4,1)} %convert_compare_fusion.2) | copy-start | bytes 786436 | tf_op jit(solution)/shard_map/while
  50.5 10.5 %copy-start.16 = (f32[2,512,128]{2,1,0:T(8,128)S(1)}, f32[2,512,128]{2,1,0:T(8,128)}, u32[]{:S(2)}) copy-start(f32[2,512,128]{2,1,0:T(8,128)} %get-tuple-element.1270) | copy-start | bytes 1572868 | tf_op jit(solution)/shard_map/while
  50.5 12.5 %copy-start.18 = (f32[2,512,128]{2,1,0:T(8,128)S(1)}, f32[2,512,128]{2,1,0:T(8,128)}, u32[]{:S(2)}) copy-start(f32[2,512,128]{2,1,0:T(8,128)} %get-tuple-element.1271) | copy-start | bytes 1572868 | tf_op jit(solution)/shard_map/while
  63.0 0.8 copy-start.17
  63.8 0.8 copy-start.19
  91.5 13.7 %copy-start.2 = (bf16[1,512,16,128]{3,2,1,0:T(8,128)(2,1)S(1)}, bf16[1,512,16,128]{3,2,1,0:T(8,128)(2,1)}, u32[]{:S(2)}) copy-start(bf16[1,512,16,128]{3,2,1,0:T(8,128)(2,1)} %get-tuple-element.1192) | copy-start | bytes 6291460 | tf_op jit(solution)/shard_map/while
  91.5 13.7 %copy-start.12 = (f32[512,512]{1,0:T(8,128)S(1)}, f32[512,512]{1,0:T(8,128)}, u32[]{:S(2)}) copy-start(f32[512,512]{1,0:T(8,128)} %fusion.168) | copy-start | bytes 3145732 | tf_op jit(solution)/shard_map/while
  91.5 13.7 %copy-start.15 = (pred[512,512]{1,0:T(8,128)(4,1)S(1)}, pred[512,512]{1,0:T(8,128)(4,1)}, u32[]{:S(2)}) copy-start(pred[512,512]{1,0:T(8,128)(4,1)} %convert_compare_fusion.2) | copy-start | bytes 786436 | tf_op jit(solution)/shard_map/while
  105.2 10.5 %copy-start.16 = (f32[2,512,128]{2,1,0:T(8,128)S(1)}, f32[2,512,128]{2,1,0:T(8,128)}, u32[]{:S(2)}) copy-start(f32[2,512,128]{2,1,0:T(8,128)} %get-tuple-element.1270) | copy-start | bytes 1572868 | tf_op jit(solution)/shard_map/while
  105.2 12.5 %copy-start.18 = (f32[2,512,128]{2,1,0:T(8,128)S(1)}, f32[2,512,128]{2,1,0:T(8,128)}, u32[]{:S(2)}) copy-start(f32[2,512,128]{2,1,0:T(8,128)} %get-tuple-element.1271) | copy-start | bytes 1572868 | tf_op jit(solution)/shard_map/while
  117.7 0.8 copy-start.17
  118.5 0.8 copy-start.19
  138.1 1.0 copy-start.7
  138.1 1.6 copy-start.13
  139.1 253.5 %all-gather.6.cloned.1.call-start = ((), (), s32[]{:S(2)}) async-start(), calls=%async_computation.4 | async-start | bytes 9437184 | tf_op jit(solution)/shard_map/all_gather | solution.py:14
  139.9 4.9 copy-start.26
  143.1 1.0 copy-start.8
  143.1 1.7 copy-start.14
  144.1 420.8 %reduce-scatter.3.cloned.1.call-start = ((), (), s32[]{:S(2)}) async-start(), calls=%async_computation.2 | async-start | bytes 655360 | tf_op jit(solution)/shard_map/reduce_scatter | solution.py:175
  429.7 4.4 copy-start.5
  434.1 1.6 copy-start.9
  445.6 5.5 copy-start.3
  455.6 11.0 %copy-start.22 = (f32[2,512,128]{2,1,0:T(8,128)S(1)}, f32[2,512,128]{2,1,0:T(8,128)}, u32[]{:S(2)}) copy-start(f32[2,512,128]{2,1,0:T(8,128)} %get-tuple-element.1420) | copy-start | bytes 1572868 | tf_op jit(solution)/shard_map/while
  461.0 5.6 copy-start.20
  461.0 6.9 %copy-start.1 = (f32[512,16,128]{2,1,0:T(8,128)S(1)}, f32[512,16,128]{2,1,0:T(8,128)}, u32[]{:S(2)}) copy-start(f32[512,16,128]{2,1,0:T(8,128)} %copy.135) | copy-start | bytes 12582916 | tf_op jit(solution)/shard_map/while
  466.6 6.1 %copy-start = (f32[512,16,128]{2,1,0:T(8,128)S(1)}, f32[512,16,128]{2,1,0:T(8,128)}, u32[]{:S(2)}) copy-start(f32[512,16,128]{2,1,0:T(8,128)} %copy.136) | copy-start | bytes 12582916 | tf_op jit(solution)/shard_map/while
  466.7 9.4 %copy-start.21 = (f32[2,512,128]{2,1,0:T(8,128)}, f32[2,512,128]{2,1,0:T(8,128)S(1)}, u32[]{:S(2)}) copy-start(f32[2,512,128]{2,1,0:T(8,128)S(1)} %get-tuple-element.1434) | copy-start | bytes 1572868 | tf_op jit(solution)/shard_map/while
  466.7 9.4 %copy-start.23 = (f32[2,512,128]{2,1,0:T(8,128)}, f32[2,512,128]{2,1,0:T(8,128)S(1)}, u32[]{:S(2)}) copy-start(f32[2,512,128]{2,1,0:T(8,128)S(1)} %get-tuple-element.1435) | copy-start | bytes 1572868 | tf_op jit(solution)/shard_map/while
  468.0 8.1 %copy-start.4 = (f32[2,16,128,128]{3,2,1,0:T(8,128)S(1)}, f32[2,16,128,128]{3,2,1,0:T(8,128)}, u32[]{:S(2)}) copy-start(f32[2,16,128,128]{3,2,1,0:T(8,128)} %get-tuple-element.1439) | copy-start | bytes 6291460 | tf_op jit(solution)/shard_map/while
  468.0 8.1 %copy-start.10 = (f32[2,16,128,128]{3,2,1,0:T(8,128)S(1)}, f32[2,16,128,128]{3,2,1,0:T(8,128)}, u32[]{:S(2)}) copy-start(f32[2,16,128,128]{3,2,1,0:T(8,128)} %get-tuple-element.1442) | copy-start | bytes 6291460 | tf_op jit(solution)/shard_map/while
  495.4 4.5 copy-start.5
  499.9 1.6 copy-start.9
  511.3 5.5 copy-start.3
  521.3 11.0 %copy-start.22 = (f32[2,512,128]{2,1,0:T(8,128)S(1)}, f32[2,512,128]{2,1,0:T(8,128)}, u32[]{:S(2)}) copy-start(f32[2,512,128]{2,1,0:T(8,128)} %get-tuple-element.1420) | copy-start | bytes 1572868 | tf_op jit(solution)/shard_map/while
  526.8 5.6 copy-start.20
  526.8 6.9 %copy-start.1 = (f32[512,16,128]{2,1,0:T(8,128)S(1)}, f32[512,16,128]{2,1,0:T(8,128)}, u32[]{:S(2)}) copy-start(f32[512,16,128]{2,1,0:T(8,128)} %copy.135) | copy-start | bytes 12582916 | tf_op jit(solution)/shard_map/while
  532.3 6.1 %copy-start = (f32[512,16,128]{2,1,0:T(8,128)S(1)}, f32[512,16,128]{2,1,0:T(8,128)}, u32[]{:S(2)}) copy-start(f32[512,16,128]{2,1,0:T(8,128)} %copy.136) | copy-start | bytes 12582916 | tf_op jit(solution)/shard_map/while
  532.4 9.4 %copy-start.21 = (f32[2,512,128]{2,1,0:T(8,128)}, f32[2,512,128]{2,1,0:T(8,128)S(1)}, u32[]{:S(2)}) copy-start(f32[2,512,128]{2,1,0:T(8,128)S(1)} %get-tuple-element.1434) | copy-start | bytes 1572868 | tf_op jit(solution)/shard_map/while
  532.4 9.4 %copy-start.23 = (f32[2,512,128]{2,1,0:T(8,128)}, f32[2,512,128]{2,1,0:T(8,128)S(1)}, u32[]{:S(2)}) copy-start(f32[2,512,128]{2,1,0:T(8,128)S(1)} %get-tuple-element.1435) | copy-start | bytes 1572868 | tf_op jit(solution)/shard_map/while
  533.7 8.1 %copy-start.4 = (f32[2,16,128,128]{3,2,1,0:T(8,128)S(1)}, f32[2,16,128,128]{3,2,1,0:T(8,128)}, u32[]{:S(2)}) copy-start(f32[2,16,128,128]{3,2,1,0:T(8,128)} %get-tuple-element.1439) | copy-start | bytes 6291460 | tf_op jit(solution)/shard_map/while
  533.8 8.1 %copy-start.10 = (f32[2,16,128,128]{3,2,1,0:T(8,128)S(1)}, f32[2,16,128,128]{3,2,1,0:T(8,128)}, u32[]{:S(2)}) copy-start(f32[2,16,128,128]{3,2,1,0:T(8,128)} %get-tuple-element.1442) | copy-start | bytes 6291460 | tf_op jit(solution)/shard_map/while
  544.9 44.7 %reduce-scatter.5.cloned.1.call-start = ((), (), s32[]{:S(2)}) async-start(), calls=%async_computation.3 | async-start | bytes 655360 | tf_op jit(solution)/shard_map/reduce_scatter | solution.py:178
Sparse Core Ops, SparseCore 0:
  139.2 128.0 all-gather.7
  269.5 123.1 all-gather.5
  545.0 19.8 reduce-scatter.2
  568.0 21.6 reduce-scatter.4
where the time goes:
time: 601 us; the launch traced here: 596 us
  waiting for transfers between devices  241 us (40%)
  matrix products  148 us (25%)
  local copies, waits for them, and re-layouts  126 us (21%)
  other arithmetic  40.9 us (7%)
  blocking collectives  23.7 us (4%)
  between operations  14.8 us (2%)
    all_gather x2, waiting for transfers between devices, prefix(): everything = jax.tree.map(lambda part: lax.all_gather(part, axis), array)  210 us
    dynamic_slice x16, local copies, waits for them, and re-layouts, on_device(): lax.map(local_block, (inputs_blocks, in_blocks, out_blocks, rate_blocks,...  31.1 us
    dot_general x2, matrix products, local_block(): jnp.einsum('hus,uhp->shp', weights, cotan_wide, precision=highest)  27.3 us
    unnamed x24, local copies, waits for them, and re-layouts  26.3 us
    reduce_scatter x1, waiting for transfers between devices, on_device(): lax.psum_scatter((out_inner + out_carried).reshape(row_count, -1), 'head'...  24.7 us
    unnamed x1, blocking collectives  23.7 us
    select_n x16, other arithmetic, hop(): return jax.tree.map(lambda a, b: jnp.where(reached, a, b), new, before)  23.5 us
    dot_general x2, matrix products, local_block(): jnp.einsum('uhp,shp->hus', cotan_blk, inputs_blk, preferred_element_type=...  21 us
  transfers between devices with their start and end apart: 4, of which 4 were waited for; matrix products, arithmetic and copies ran while one was open for 5% of the time, Pallas kernels for 0%

commit v1 on v0

v1 whole, which is shorter than its diff:
```python
import functools

import jax
import jax.numpy as jnp
from jax import lax
from jax.experimental import pallas as pl
from jax.experimental.pallas import tpu as pltpu
from jax.sharding import PartitionSpec as P

MESH = pl.DeviceIdType.MESH
F32, BF16 = jnp.float32, jnp.bfloat16
HIGHEST = lax.Precision.HIGHEST
CHUNK = 128
GROUP = 4
SPLIT = 2
SKEW = 2
VMEM_BYTES = 56 * 1024 * 1024


def nn(a, b, **kw):
    return lax.dot_general(a, b, (((1,), (0,)), ((), ())), preferred_element_type=F32, **kw)


def nt(a, b, **kw):
    return lax.dot_general(a, b, (((1,), (1,)), ((), ())), preferred_element_type=F32, **kw)


def tn(a, b, **kw):
    return lax.dot_general(a, b, (((0,), (0,)), ((), ())), preferred_element_type=F32, **kw)


def split(v):
    hi = v.astype(BF16)
    return hi, (v - hi.astype(F32)).astype(BF16)


def order(strict=False):
    row = lax.broadcasted_iota(jnp.int32, (CHUNK, CHUNK), 0)
    col = lax.broadcasted_iota(jnp.int32, (CHUNK, CHUNK), 1)
    return row > col if strict else row >= col


def wide(v, width):
    rows, heads = v.shape
    return jnp.concatenate(
        [jnp.broadcast_to(v[:, h : h + 1], (rows, width)) for h in range(heads)], axis=1
    )


def decays(rates):
    run = nt(order().astype(F32), rates, precision=HIGHEST)
    mid = run[CHUNK // 2 - 1 : CHUNK // 2, :]
    f = jnp.exp(run - mid)
    return f, jnp.exp(mid - run), jnp.exp(mid), f[CHUNK - 1 : CHUNK, :]


def heads_of(v, width):
    return [v[:, h : h + width] for h in range(0, v.shape[1], width)]


def states_kernel(x_ref, b_ref, c_ref, rate_ref, dy_ref, s_ref, e_ref, total_ref):
    tokens, columns = x_ref.shape
    width = columns // rate_ref.shape[1]
    chunks = tokens // CHUNK
    state = adjoint = jnp.zeros((b_ref.shape[1], columns), F32)
    reach = jnp.ones((1, columns), F32)
    for j in range(chunks):
        rows = pl.ds(j * CHUNK, CHUNK)
        f, g, mid, last = decays(rate_ref[0, :, rows])
        mid, last = wide(mid, width), wide(last, width)
        b, c = b_ref[rows, :], c_ref[rows, :]
        gx_hi, gx_lo = split(wide(g, width) * x_ref[rows, :].astype(F32))
        fy_hi, fy_lo = split(wide(f, width) * dy_ref[rows, :].astype(F32))
        state = (last * mid) * state + last * (tn(b, gx_hi) + tn(b, gx_lo))
        adjoint = adjoint + (reach * mid) * (tn(c, fy_hi) + tn(c, fy_lo))
        reach = reach * (last * mid)
    for h, (s, e, r) in enumerate(
        zip(heads_of(state, width), heads_of(adjoint, width), heads_of(reach, width))
    ):
        s_ref[h] = s
        e_ref[h] = e
        total_ref[h] = jnp.broadcast_to(r, total_ref.shape[1:])


def chain_kernel(
    peers, s_ref, e_ref, total_ref, s_in, e_in, s_out, e_out, s_send, s_recv, e_send, e_recv
):
    me, lane = lax.axis_index("seq"), lax.axis_index("head")
    items = s_ref.shape[0]
    has_left, has_right = me > 0, me < peers - 1
    barrier = pltpu.get_barrier_semaphore()

    @pl.when(has_left)
    def _():
        pl.semaphore_signal(barrier, inc=1, device_id=(me - 1, lane), device_id_type=MESH)

    @pl.when(has_right)
    def _():
        pl.semaphore_signal(barrier, inc=1, device_id=(me + 1, lane), device_id_type=MESH)

    pl.semaphore_wait(barrier, jnp.where(has_left, 1, 0) + jnp.where(has_right, 1, 0))

    def forward(i):
        return pltpu.make_async_remote_copy(
            src_ref=s_out.at[i], dst_ref=s_in.at[i], send_sem=s_send.at[i], recv_sem=s_recv.at[i],
            device_id=(me + 1, lane), device_id_type=MESH,
        )

    def backward(i):
        return pltpu.make_async_remote_copy(
            src_ref=e_out.at[i], dst_ref=e_in.at[i], send_sem=e_send.at[i], recv_sem=e_recv.at[i],
            device_id=(me - 1, lane), device_id_type=MESH,
        )

    def pass_on(i, copy, has_source, has_target, local, come, out):
        @pl.when(has_source)
        def _():
            copy(i).wait_recv()

        @pl.when(jnp.logical_not(has_source))
        def _():
            come[i] = jnp.zeros(come.shape[1:], F32)

        @pl.when(has_target)
        def _():
            out[i] = total_ref[i // SPLIT][0:1, :] * come[i] + local[i]
            copy(i).start()

    def step(i, _):
        at_s, at_e = i - SKEW * me, i - SKEW * (peers - 1 - me)

        @pl.when(jnp.logical_and(at_s >= 0, at_s < items))
        def _():
            pass_on(at_s, forward, has_left, has_right, s_ref, s_in, s_out)

        @pl.when(jnp.logical_and(at_e >= 0, at_e < items))
        def _():
            pass_on(at_e, backward, has_right, has_left, e_ref, e_in, e_out)

        return 0

    lax.fori_loop(0, items + SKEW * (peers - 1), step, 0)

    def finish(i, _):
        @pl.when(has_right)
        def _():
            forward(i).wait_send()

        @pl.when(has_left)
        def _():
            backward(i).wait_send()

        return 0

    lax.fori_loop(0, items, finish, 0)


def grads_kernel(
    x_ref, b_ref, c_ref, rate_ref, dy_ref, s_ref, e_ref,
    gx_ref, gb_ref, gc_ref, rates_out, adjoints, fy_hi_ref, fy_lo_ref, joint,
):
    group = pl.program_id(0)
    tokens, columns = x_ref.shape
    heads = rate_ref.shape[1]
    width = columns // heads
    chunks = tokens // CHUNK
    causal = order()
    after = jnp.logical_not(order()).astype(F32)
    head_lane = lax.broadcasted_iota(jnp.int32, (CHUNK, heads), 1)

    @pl.when(group == 0)
    def _():
        gb_ref[...] = jnp.zeros_like(gb_ref)
        gc_ref[...] = jnp.zeros_like(gc_ref)
        joint[...] = jnp.zeros_like(joint)

    def per_head(v):
        out = jnp.zeros((CHUNK, heads), F32)
        for h, part in enumerate(heads_of(v, width)):
            out = jnp.where(head_lane == h, jnp.sum(part, axis=1, keepdims=True), out)
        return out

    adjoint = jnp.concatenate([e_ref[h] for h in range(heads)], axis=1)
    adjoints[chunks] = adjoint
    for j in reversed(range(chunks)):
        rows = pl.ds(j * CHUNK, CHUNK)
        f, g, mid, last = decays(rate_ref[0, :, rows])
        mid, last = wide(mid, width), wide(last, width)
        fy_hi, fy_lo = split(wide(f, width) * dy_ref[rows, :].astype(F32))
        fy_hi_ref[rows, :] = fy_hi
        fy_lo_ref[rows, :] = fy_lo
        c = c_ref[rows, :]
        adjoint = mid * (last * adjoint + (tn(c, fy_hi) + tn(c, fy_lo)))
        adjoints[j] = adjoint

    state = jnp.concatenate([s_ref[h] for h in range(heads)], axis=1)
    for j in range(chunks):
        rows = pl.ds(j * CHUNK, CHUNK)
        f, g, mid, last = decays(rate_ref[0, :, rows])
        mid, last = wide(mid, width), wide(last, width)
        g_wide = wide(g, width)
        b, c = b_ref[rows, :], c_ref[rows, :]
        gx = g_wide * x_ref[rows, :].astype(F32)
        gx_hi, gx_lo = split(gx)
        fy_hi, fy_lo = fy_hi_ref[rows, :], fy_lo_ref[rows, :]
        scores = jnp.where(causal, nt(c, b), 0.0)
        m_hi, m_lo = split(scores)
        t_hi, t_lo = split(scores.T)
        s_hi, s_lo = split(mid * state)
        e_hi, e_lo = split(last * adjoints[j + 1])
        y = nn(
            jnp.concatenate([m_hi, m_hi, m_lo, c, c], axis=1),
            jnp.concatenate([gx_hi, gx_lo, gx_hi, s_hi, s_lo], axis=0),
        )
        z = nn(
            jnp.concatenate([t_hi, t_hi, t_lo, b, b], axis=1),
            jnp.concatenate([fy_hi, fy_lo, fy_hi, e_hi, e_lo], axis=0),
        )
        gx_ref[rows, :] = g_wide * z
        fy = fy_hi.astype(F32) + fy_lo.astype(F32)
        turnover = per_head(gx * z - fy * y)
        crossing = per_head(adjoints[j] * state)
        rates_out[0, :, rows] = tn(turnover, after, precision=HIGHEST) + tn(
            crossing, jnp.ones((CHUNK, CHUNK), F32), precision=HIGHEST
        )
        both = nt(
            jnp.concatenate([fy_hi, fy_hi, fy_lo], axis=1),
            jnp.concatenate(
                [
                    jnp.concatenate([s_hi, s_lo, s_hi], axis=1),
                    jnp.concatenate([gx_hi, gx_lo, gx_hi], axis=1),
                ],
                axis=0,
            ),
        )
        n = s_hi.shape[0]
        gc_ref[rows, :] += both[:, :n]
        joint[j] += both[:, n:]
        gb_ref[rows, :] += nt(
            jnp.concatenate([gx_hi, gx_hi, gx_lo], axis=1),
            jnp.concatenate([e_hi, e_lo, e_hi], axis=1),
        )
        state = last * (mid * state + (tn(b, gx_hi) + tn(b, gx_lo)))

    @pl.when(group == pl.num_programs(0) - 1)
    def _():
        for j in range(chunks):
            rows = pl.ds(j * CHUNK, CHUNK)
            b, c = b_ref[rows, :], c_ref[rows, :]
            j_hi, j_lo = split(jnp.where(causal, joint[j], 0.0))
            gc_ref[rows, :] += nn(j_hi, b) + nn(j_lo, b)
            gb_ref[rows, :] += tn(j_hi, c) + tn(j_lo, c)


def on_device(peers, inputs, in_map, out_map, log_decay, cotangent):
    heads, tokens = log_decay.shape
    width = inputs.shape[1] // heads
    states = in_map.shape[1]
    groups = heads // GROUP
    columns = GROUP * width
    rates = log_decay.reshape(groups, GROUP, tokens)
    vmem = pl.BlockSpec(memory_space=pltpu.VMEM)
    channel_block = pl.BlockSpec((tokens, columns), lambda i: (0, i))
    map_block = pl.BlockSpec((tokens, states), lambda i: (0, 0))
    rate_block = pl.BlockSpec((1, GROUP, tokens), lambda i: (i, 0, 0))
    state_block = pl.BlockSpec((GROUP, states, width), lambda i: (i, 0, 0))
    state_shape = jax.ShapeDtypeStruct((heads, states, width), F32)
    params = pltpu.CompilerParams(
        dimension_semantics=("arbitrary",), vmem_limit_bytes=VMEM_BYTES
    )
    s_here, e_here, totals = pl.pallas_call(
        states_kernel,
        grid=(groups,),
        in_specs=[channel_block, map_block, map_block, rate_block, channel_block],
        out_specs=[state_block, state_block, pl.BlockSpec((GROUP, 8, width), lambda i: (i, 0, 0))],
        out_shape=[state_shape, state_shape, jax.ShapeDtypeStruct((heads, 8, width), F32)],
        compiler_params=params,
        name="shard_states",
    )(inputs, in_map, out_map, rates, cotangent)

    items = heads * SPLIT
    message = (items, states // SPLIT, width)
    message_shape = jax.ShapeDtypeStruct(message, F32)
    s_in, e_in = pl.pallas_call(
        functools.partial(chain_kernel, peers),
        in_specs=[vmem, vmem, vmem],
        out_specs=[vmem, vmem],
        out_shape=[message_shape, message_shape],
        scratch_shapes=[
            pltpu.VMEM(message, F32),
            pltpu.VMEM(message, F32),
            pltpu.SemaphoreType.DMA((items,)),
            pltpu.SemaphoreType.DMA((items,)),
            pltpu.SemaphoreType.DMA((items,)),
            pltpu.SemaphoreType.DMA((items,)),
        ],
        compiler_params=pltpu.CompilerParams(
            collective_id=0, has_side_effects=True, vmem_limit_bytes=VMEM_BYTES
        ),
        name="carry_chain",
    )(s_here.reshape(message), e_here.reshape(message), totals)
    s_in = s_in.reshape(heads, states, width)
    e_in = e_in.reshape(heads, states, width)

    map_shape = jax.ShapeDtypeStruct((tokens, states), F32)
    chunks = tokens // CHUNK
    grad_inputs, grad_in, grad_out, grad_rates = pl.pallas_call(
        grads_kernel,
        grid=(groups,),
        in_specs=[
            channel_block, map_block, map_block, rate_block, channel_block, state_block, state_block
        ],
        out_specs=[channel_block, map_block, map_block, rate_block],
        out_shape=[
            jax.ShapeDtypeStruct(inputs.shape, F32),
            map_shape,
            map_shape,
            jax.ShapeDtypeStruct(rates.shape, F32),
        ],
        scratch_shapes=[
            pltpu.VMEM((chunks + 1, states, columns), F32),
            pltpu.VMEM((tokens, columns), BF16),
            pltpu.VMEM((tokens, columns), BF16),
            pltpu.VMEM((chunks, CHUNK, CHUNK), F32),
        ],
        compiler_params=params,
        name="gradients",
    )(inputs, in_map, out_map, rates, cotangent, s_in, e_in)

    grad_in, grad_out = (
        lax.psum_scatter(g, "head", scatter_dimension=0, tiled=True) for g in (grad_in, grad_out)
    )
    return grad_inputs, grad_in, grad_out, grad_rates.reshape(heads, tokens)


def solution(mesh):
    placed = (P("seq", "head"), P("seq", None), P("seq", None), P("head", "seq"), P("seq", "head"))
    return jax.shard_map(
        functools.partial(on_device, mesh.shape["seq"]),
        mesh=mesh,
        in_specs=placed,
        out_specs=(
            P("seq", "head"),
            P(("seq", "head"), None),
            P(("seq", "head"), None),
            P("head", "seq"),
        ),
        check_vma=False,
    )
```

time: 601 us -> 214 us (0.36)
  waiting for transfers between devices: 241 us -> 44.5 us
  Pallas kernels: 0 us -> 152 us
  matrix products: 148 us -> 0 us
  local copies, waits for them, and re-layouts: 126 us -> 2.98 us
  other arithmetic: 40.9 us -> 0 us
  blocking collectives: 23.7 us -> 0 us
    all_gather x2 -> x0, waiting for transfers between devices: 210 us -> none  [prefix(): everything = jax.tree.map(lambda part: lax.all_gather(part, axis), array)]
    pallas_call x0 -> x3, Pallas kernels: none -> 152 us  [the longest x1 82 us: on_device(): pl.pallas_call(functools.partial(chain_kernel, peers), in_specs=[vmem, vm...]
    dot_general x38 -> x0, matrix products: 148 us -> none  [the longest x2 27.3 us: local_block(): jnp.einsum('hus,uhp->shp', weights, cotan_wide, precision=highest)]
    dynamic_slice x20 -> x0, local copies, waits for them, and re-layouts: 51.2 us -> none  [the longest x16 31.1 us: on_device(): lax.map(local_block, (inputs_blocks, in_blocks, out_blocks, rate_blocks,...]
    unnamed x24 -> x0, local copies, waits for them, and re-layouts: 26.3 us -> none
    unnamed x1 -> x0, blocking collectives: 23.7 us -> none
    select_n x16 -> x0, other arithmetic: 23.5 us -> none  [hop(): return jax.tree.map(lambda a, b: jnp.where(reached, a, b), new, before)]
    transpose x6 -> x0, local copies, waits for them, and re-layouts: 22.1 us -> none  [the longest x2 11 us: carried_block(): jnp.einsum('thp,hpn->thn', inputs_wide, end_adjoint, precision=highest)]
  transfers between devices with their start and end apart: 4 -> 2, of which waited for: 4 -> 2; matrix products, arithmetic and copies ran while one was open for 5% -> 1% of each run, Pallas kernels for 0% -> 0%
where the time goes in v1:
time: 214 us
  Pallas kernels  152 us (71%)
  waiting for transfers between devices  44.5 us (21%)
  between operations  14 us (7%)
  local copies, waits for them, and re-layouts  2.98 us (1%)
    pallas_call x1, Pallas kernels, on_device(): pl.pallas_call(functools.partial(chain_kernel, peers), in_specs=[vmem, vm...  82 us
    pallas_call x1, Pallas kernels, on_device(): pl.pallas_call(grads_kernel, grid=(groups,), in_specs=[channel_block, map...  50.6 us
    reduce_scatter x2, waiting for transfers between devices, on_device(): lax.psum_scatter(g, 'head', scatter_dimension=0, tiled=True)  43.8 us
    pallas_call x1, Pallas kernels, on_device(): pl.pallas_call(states_kernel, grid=(groups,), in_specs=[channel_block, ma...  19.7 us
  transfers between devices with their start and end apart: 2, of which 2 were waited for; matrix products, arithmetic and copies ran while one was open for 1% of the time, Pallas kernels for 0%

profile of v1, /device:TPU:0, one launch (start us, length us, event | category | flops | bytes accessed | tf_op | source)
XLA Modules:
  0.0 213.9 jit_solution(8741129721206928715)
XLA Ops:
  7.2 0.0 reduce-scatter.3.cloned.1.call-start
  7.2 1.5 reshape.26.rate_ref
  8.7 19.7 %shard_states.1 = (f32[16,128,128]{2,1,0:T(8,128)}, f32[16,128,128]{2,1,0:T(8,128)}, f32[16,8,128]{2,1,0:T(8,128)}) custom-call(bf16[1024,2048]{1,0:T(8,128)(2,1)} %x_ref.3, bf16[1024,128]{1,0:T(8,128)(2,1)} %b_ref.3, bf16[1024,128]{1,0:T(8,128)(2,1)} %c_ref.3, f32[4,4,1024]{2,1,0:T(4,128)} %reshape.26.rate_ref, bf16[1024,2048]{1,0:T(8,128)(2,1)} %dy_ref.3), custom_call_target="tpu_custom_call" | custom-call | tf_op jit(solution)/shard_map/shard_states/pallas_call | solution.py:271
  28.4 82.0 %carry_chain.1 = (f32[32,64,128]{2,1,0:T(8,128)}, f32[32,64,128]{2,1,0:T(8,128)}) custom-call(f32[32,64,128]{2,1,0:T(8,128)} %bitcast.4, f32[32,64,128]{2,1,0:T(8,128)} %bitcast.5, f32[16,8,128]{2,1,0:T(8,128)} %get-tuple-element.15.total_ref), custom_call_target="tpu_custom_call" | custom-call | tf_op jit(solution)/shard_map/carry_chain/pallas_call | solution.py:284
  110.5 50.6 %gradients.1 = (f32[1024,2048]{1,0:T(8,128)}, f32[1024,128]{1,0:T(8,128)}, f32[1024,128]{1,0:T(8,128)}, f32[4,4,1024]{2,1,0:T(4,128)}) custom-call(bf16[1024,2048]{1,0:T(8,128)(2,1)} %x_ref.3, bf16[1024,128]{1,0:T(8,128)(2,1)} %b_ref.3, bf16[1024,128]{1,0:T(8,128)(2,1)} %c_ref.3, f32[4,4,1024]{2,1,0:T(4,128)} %reshape.26.rate_ref, ...), custom_call_target="tpu_custom_call" | custom-call | tf_op jit(solution)/shard_map/gradients/pallas_call | solution.py:307
  161.1 0.0 reduce-scatter.3.cloned.1.call-update
  161.1 0.0 reduce-scatter.5.cloned.1.call-start
  161.1 0.7 reduce-scatter.5.cloned.1.call-update
  161.8 1.5 reshape.31
  163.3 18.9 %reduce-scatter.3.cloned.1.call-done = f32[256,128]{1,0:T(8,128)} async-done(((f32[1024,128]{1,0:T(8,128)}), f32[256,128]{1,0:T(8,128)}) %reduce-scatter.3.cloned.1.call-update) | async-done | bytes 131088 | tf_op jit(solution)/shard_map/reduce_scatter | solution.py:331
  182.2 24.9 %reduce-scatter.5.cloned.1.call-done = f32[256,128]{1,0:T(8,128)} async-done(((f32[1024,128]{1,0:T(8,128)}), f32[256,128]{1,0:T(8,128)}) %reduce-scatter.5.cloned.1.call-update) | async-done | bytes 131088 | tf_op jit(solution)/shard_map/reduce_scatter | solution.py:331
Async XLA Ops:
  7.2 175.0 %reduce-scatter.3.cloned.1.call-start = ((), (), s32[]{:S(2)}) async-start(), calls=%async_computation.2 | async-start | bytes 655360 | tf_op jit(solution)/shard_map/reduce_scatter | solution.py:331
  161.1 46.0 %reduce-scatter.5.cloned.1.call-start = ((), (), s32[]{:S(2)}) async-start(), calls=%async_computation.3 | async-start | bytes 655360 | tf_op jit(solution)/shard_map/reduce_scatter | solution.py:331
Sparse Core Ops, SparseCore 0:
  161.2 20.9 reduce-scatter.2
  185.4 21.6 reduce-scatter.4

commit v2 on v1

v2 whole, which is shorter than its diff:
```python
import functools

import jax
import jax.numpy as jnp
from jax import lax
from jax.experimental import pallas as pl
from jax.experimental.pallas import tpu as pltpu
from jax.sharding import PartitionSpec as P

MESH = pl.DeviceIdType.MESH
F32, BF16 = jnp.float32, jnp.bfloat16
HIGHEST = lax.Precision.HIGHEST
CHUNK = 128
GROUP = 4
SPLIT = 2
SKEW = 2
VMEM_BYTES = 56 * 1024 * 1024


def nn(a, b, **kw):
    return lax.dot_general(a, b, (((1,), (0,)), ((), ())), preferred_element_type=F32, **kw)


def nt(a, b, **kw):
    return lax.dot_general(a, b, (((1,), (1,)), ((), ())), preferred_element_type=F32, **kw)


def tn(a, b, **kw):
    return lax.dot_general(a, b, (((0,), (0,)), ((), ())), preferred_element_type=F32, **kw)


def split(v):
    hi = v.astype(BF16)
    return hi, (v - hi.astype(F32)).astype(BF16)


def order():
    row = lax.broadcasted_iota(jnp.int32, (CHUNK, CHUNK), 0)
    col = lax.broadcasted_iota(jnp.int32, (CHUNK, CHUNK), 1)
    return row >= col


def wide(v, width):
    rows, heads = v.shape
    return jnp.concatenate(
        [jnp.broadcast_to(v[:, h : h + 1], (rows, width)) for h in range(heads)], axis=1
    )


def heads_of(v, width):
    return [v[:, h : h + width] for h in range(0, v.shape[1], width)]


def per_head(v, heads):
    rows = v.shape[0]
    lane = lax.broadcasted_iota(jnp.int32, (rows, heads), 1)
    out = jnp.zeros((rows, heads), F32)
    for h, part in enumerate(heads_of(v, v.shape[1] // heads)):
        out = jnp.where(lane == h, jnp.sum(part, axis=1, keepdims=True), out)
    return out


def running_of(rates):
    upper = jnp.logical_not(order()).astype(F32) + (
        lax.broadcasted_iota(jnp.int32, (CHUNK, CHUNK), 0)
        == lax.broadcasted_iota(jnp.int32, (CHUNK, CHUNK), 1)
    ).astype(F32)
    return nn(rates, upper, precision=HIGHEST)


def shard_decays(rates, heads):
    rows = rates.shape[0]
    run = running_of(rates)
    row = lax.broadcasted_iota(jnp.int32, (rows, rows), 0)
    col = lax.broadcasted_iota(jnp.int32, (rows, rows), 1)
    same = lax.rem(row, heads) == lax.rem(col, heads)
    last = run[:, CHUNK - 1 : CHUNK]
    wide_last = jnp.broadcast_to(last, run.shape)
    earlier = nn(jnp.logical_and(same, col < row).astype(F32), wide_last, precision=HIGHEST)
    later = nn(jnp.logical_and(same, col > row).astype(F32), wide_last, precision=HIGHEST)
    from_start = (jnp.exp(earlier) * jnp.exp(run)).T
    to_end = jnp.exp(later + (last - run)).T
    return from_start, to_end, from_start[CHUNK - 1 : CHUNK, rows - heads :]


def states_kernel(x_ref, b_ref, c_ref, rate_ref, dy_ref, s_ref, e_ref, total_ref):
    tokens, columns = x_ref.shape
    heads, width = s_ref.shape[0], s_ref.shape[2]
    from_start, to_end, total = shard_decays(rate_ref[0], heads)

    def scaled(ref, factors):
        parts = []
        for j in range(tokens // CHUNK):
            rows = pl.ds(j * CHUNK, CHUNK)
            cols = factors[:, j * heads : (j + 1) * heads]
            parts.append(split(wide(cols, width) * ref[rows, :].astype(F32)))
        return jnp.concatenate([hi for hi, _ in parts] + [lo for _, lo in parts], axis=0)

    def twice(ref):
        turned = ref[...].T
        return jnp.concatenate([turned, turned], axis=1)

    state = nn(twice(b_ref), scaled(x_ref, to_end))
    adjoint = nn(twice(c_ref), scaled(dy_ref, from_start))
    for h, (s, e) in enumerate(zip(heads_of(state, width), heads_of(adjoint, width))):
        s_ref[h] = s
        e_ref[h] = e
        total_ref[h] = jnp.broadcast_to(total[:, h : h + 1], total_ref.shape[1:])


def chain_kernel(
    peers, groups, s_ref, e_ref, total_ref, x_ref, b_ref, c_ref, rate_ref, dy_ref,
    s_in, e_in, gx_ref, gb_ref, gc_ref, rates_out,
    s_out, e_out, s_send, s_recv, e_send, e_recv,
    f_ref, g_ref, end_ref, scores_ref, adjoints, fy_hi_ref, fy_lo_ref, state_ref, joint,
):
    me, lane = lax.axis_index("seq"), lax.axis_index("head")
    items = s_ref.shape[0]
    has_left, has_right = me > 0, me < peers - 1
    barrier = pltpu.get_barrier_semaphore()

    @pl.when(has_left)
    def _():
        pl.semaphore_signal(barrier, inc=1, device_id=(me - 1, lane), device_id_type=MESH)

    @pl.when(has_right)
    def _():
        pl.semaphore_signal(barrier, inc=1, device_id=(me + 1, lane), device_id_type=MESH)

    pl.semaphore_wait(barrier, jnp.where(has_left, 1, 0) + jnp.where(has_right, 1, 0))

    def forward(i):
        return pltpu.make_async_remote_copy(
            src_ref=s_out.at[i], dst_ref=s_in.at[i], send_sem=s_send.at[i], recv_sem=s_recv.at[i],
            device_id=(me + 1, lane), device_id_type=MESH,
        )

    def backward(i):
        return pltpu.make_async_remote_copy(
            src_ref=e_out.at[i], dst_ref=e_in.at[i], send_sem=e_send.at[i], recv_sem=e_recv.at[i],
            device_id=(me - 1, lane), device_id_type=MESH,
        )

    def pass_on(i, copy, has_source, has_target, local, come, out):
        @pl.when(has_source)
        def _():
            copy(i).wait_recv()

        @pl.when(jnp.logical_not(has_source))
        def _():
            come[i] = jnp.zeros(come.shape[1:], F32)

        @pl.when(has_target)
        def _():
            out[i] = total_ref[i // SPLIT][0:1, :] * come[i] + local[i]
            copy(i).start()


    tokens = x_ref.shape[0]
    chunks = tokens // CHUNK
    width = s_ref.shape[2]
    heads = rate_ref.shape[1] // chunks
    columns = heads * width
    states = b_ref.shape[1]
    pairs = chunks // 2
    period = chunks + pairs
    causal = order()
    after = jnp.logical_not(causal).astype(F32)

    gb_ref[...] = jnp.zeros_like(gb_ref)
    gc_ref[...] = jnp.zeros_like(gc_ref)
    joint[...] = jnp.zeros_like(joint)

    def prepare(group):
        run = running_of(rate_ref[group])
        mid = run[:, CHUNK // 2 - 1 : CHUNK // 2]
        f = jnp.exp(run - mid)
        f_cols, g_cols = f.T, jnp.exp(mid - run).T
        m_cols = jnp.broadcast_to(jnp.exp(mid), run.shape).T
        for j in range(chunks):
            at = slice(j * heads, (j + 1) * heads)
            f_ref[j] = f_cols[:, at]
            g_ref[j] = g_cols[:, at]
            end_ref[j, 0:1, :] = wide(m_cols[0:1, at], width)
            end_ref[j, 1:2, :] = wide(f_cols[CHUNK - 1 : CHUNK, at], width)

    def scores_of(j, _):
        rows = pl.ds(pl.multiple_of(j * CHUNK, CHUNK), CHUNK)
        scores = jnp.where(causal, nt(c_ref[rows, :], b_ref[rows, :]), 0.0)
        for k, part in enumerate(split(scores) + split(scores.T)):
            scores_ref[j, k] = part
        return 0

    def backward_chunk(group, j):
        rows = pl.ds(pl.multiple_of(j * CHUNK, CHUNK), CHUNK)
        cols = pl.ds(pl.multiple_of(group * columns, columns), columns)
        mid, last = end_ref[j, 0:1, :], end_ref[j, 1:2, :]
        fy_hi, fy_lo = split(wide(f_ref[j], width) * dy_ref[rows, cols].astype(F32))
        fy_hi_ref[rows, :] = fy_hi
        fy_lo_ref[rows, :] = fy_lo
        c = c_ref[rows, :].T
        part = nn(jnp.concatenate([c, c], axis=1), jnp.concatenate([fy_hi, fy_lo], axis=0))
        adjoints[j] = mid * (last * adjoints[j + 1] + part)

    def forward_chunk(group, j):
        rows = pl.ds(pl.multiple_of(j * CHUNK, CHUNK), CHUNK)
        cols = pl.ds(pl.multiple_of(group * columns, columns), columns)
        mid, last = end_ref[j, 0:1, :], end_ref[j, 1:2, :]
        g_wide = wide(g_ref[j], width)
        b, c = b_ref[rows, :], c_ref[rows, :]
        gx = g_wide * x_ref[rows, cols].astype(F32)
        gx_hi, gx_lo = split(gx)
        fy_hi, fy_lo = fy_hi_ref[rows, :], fy_lo_ref[rows, :]
        m_hi, m_lo, t_hi, t_lo = (scores_ref[j, k] for k in range(4))
        state = state_ref[...]
        s_hi, s_lo = split(mid * state)
        e_hi, e_lo = split(last * adjoints[j + 1])
        y = nn(
            jnp.concatenate([m_hi, m_hi, m_lo, c, c], axis=1),
            jnp.concatenate([gx_hi, gx_lo, gx_hi, s_hi, s_lo], axis=0),
        )
        z = nn(
            jnp.concatenate([t_hi, t_hi, t_lo, b, b], axis=1),
            jnp.concatenate([fy_hi, fy_lo, fy_hi, e_hi, e_lo], axis=0),
        )
        gx_ref[rows, cols] = g_wide * z
        fy = fy_hi.astype(F32) + fy_lo.astype(F32)
        turnover = per_head(gx * z - fy * y, heads)
        crossing = per_head(adjoints[j] * state, heads)
        rates_out[group * chunks + j] = tn(turnover, after, precision=HIGHEST) + tn(
            crossing, jnp.ones((states, CHUNK), F32), precision=HIGHEST
        )
        both = nt(
            jnp.concatenate([fy_hi, fy_hi, fy_lo], axis=1),
            jnp.concatenate(
                [
                    jnp.concatenate([s_hi, s_lo, s_hi], axis=1),
                    jnp.concatenate([gx_hi, gx_lo, gx_hi], axis=1),
                ],
                axis=0,
            ),
        )
        gc_ref[rows, :] += both[:, :states]
        joint[j] += both[:, states:]
        gb_ref[rows, :] += nt(
            jnp.concatenate([gx_hi, gx_hi, gx_lo], axis=1),
            jnp.concatenate([e_hi, e_lo, e_hi], axis=1),
        )
        turned = b.T
        part = nn(jnp.concatenate([turned, turned], axis=1), jnp.concatenate([gx_hi, gx_lo], axis=0))
        state_ref[...] = last * (mid * state + part)

    def work(i):
        group, at = i // period, lax.rem(i, period)

        @pl.when(at == 0)
        def _():
            prepare(group)
            adjoints[chunks] = jnp.zeros((states, columns), F32)
            state_ref[...] = jnp.zeros_like(state_ref)

        @pl.when(at < pairs)
        def _():
            backward_chunk(group, chunks - 1 - 2 * at)
            backward_chunk(group, chunks - 2 - 2 * at)

        @pl.when(at >= pairs)
        def _():
            forward_chunk(group, at - pairs)

    def step(i, _):
        at_s, at_e = i - SKEW * me, i - SKEW * (peers - 1 - me)

        @pl.when(jnp.logical_and(at_s >= 0, at_s < items))
        def _():
            pass_on(at_s, forward, has_left, has_right, s_ref, s_in, s_out)

        @pl.when(jnp.logical_and(at_e >= 0, at_e < items))
        def _():
            pass_on(at_e, backward, has_right, has_left, e_ref, e_in, e_out)

        @pl.when(i == 0)
        def _():
            lax.fori_loop(0, chunks, scores_of, 0)

        @pl.when(i < groups * period)
        def _():
            work(i)

        return 0

    lax.fori_loop(0, max(items + SKEW * (peers - 1), groups * period), step, 0)

    def inner(j, _):
        rows = pl.ds(pl.multiple_of(j * CHUNK, CHUNK), CHUNK)
        b, c = b_ref[rows, :], c_ref[rows, :]
        j_hi, j_lo = split(jnp.where(causal, joint[j], 0.0))
        gc_ref[rows, :] += nn(j_hi, b) + nn(j_lo, b)
        gb_ref[rows, :] += tn(j_hi, c) + tn(j_lo, c)
        return 0

    lax.fori_loop(0, chunks, inner, 0)

    def finish(i, _):
        @pl.when(has_right)
        def _():
            forward(i).wait_send()

        @pl.when(has_left)
        def _():
            backward(i).wait_send()

        return 0

    lax.fori_loop(0, items, finish, 0)


def carried_kernel(
    x_ref, b_ref, c_ref, rate_ref, dy_ref, s_ref, e_ref, gx_here, gb_here, gc_here, rates_here,
    gx_ref, gb_ref, gc_ref, rates_out,
):
    tokens, columns = x_ref.shape
    heads, states, width = s_ref.shape
    chunks = tokens // CHUNK
    from_start, to_end, total = shard_decays(rate_ref[0], heads)
    causal = order()
    ordered = jnp.concatenate(
        [causal.astype(F32), jnp.logical_not(causal).astype(F32), jnp.ones((states, CHUNK), F32)],
        axis=0,
    )

    @pl.when(pl.program_id(0) == 0)
    def _():
        gb_ref[...] = gb_here[...]
        gc_ref[...] = gc_here[...]

    s_all = [s_ref[h] for h in range(heads)]
    e_all = [e_ref[h] for h in range(heads)]
    crossing = per_head(jnp.concatenate([s * e for s, e in zip(s_all, e_all)], axis=1), heads) * total
    s_parts = [jnp.concatenate(split(s), axis=1) for s in s_all]
    e_parts = [jnp.concatenate(split(e), axis=1) for e in e_all]
    e_rows = jnp.concatenate(split(jnp.concatenate(e_all, axis=1)), axis=0)
    lane = lax.broadcasted_iota(jnp.int32, (CHUNK, heads), 1)
    outs, ins = [], []
    for j in range(chunks):
        rows = pl.ds(j * CHUNK, CHUNK)
        at = slice(j * heads, (j + 1) * heads)
        fs, te = from_start[:, at], to_end[:, at]
        b, c = b_ref[rows, :], c_ref[rows, :]
        b_wide, c_wide = b.astype(F32), c.astype(F32)
        z = nn(jnp.concatenate([b, b], axis=1), e_rows)
        gb, gc = gb_ref[rows, :], gc_ref[rows, :]
        d_out = d_in = jnp.zeros((CHUNK, heads), F32)
        for h in range(heads):
            here = slice(h * width, (h + 1) * width)
            x, dy = x_ref[rows, here], dy_ref[rows, here]
            fs_h = jnp.broadcast_to(fs[:, h : h + 1], (CHUNK, width))
            te_h = jnp.broadcast_to(te[:, h : h + 1], (CHUNK, width))
            gx_ref[rows, here] = gx_here[rows, here] + te_h * z[:, here]
            feed_out = fs_h * nt(jnp.concatenate([dy, dy], axis=1), s_parts[h])
            feed_in = te_h * nt(jnp.concatenate([x, x], axis=1), e_parts[h])
            gc += feed_out
            gb += feed_in
            d_out = jnp.where(lane == h, jnp.sum(feed_out * c_wide, axis=1, keepdims=True), d_out)
            d_in = jnp.where(lane == h, jnp.sum(feed_in * b_wide, axis=1, keepdims=True), d_in)
        gb_ref[rows, :] = gb
        gc_ref[rows, :] = gc
        outs.append(d_out)
        ins.append(d_in)
    for j in range(chunks):
        beyond = crossing + sum(outs[j + 1 :]) + sum(ins[:j])
        terms = jnp.concatenate([outs[j], ins[j], beyond], axis=0)
        rates_out[0, :, pl.ds(j * CHUNK, CHUNK)] = rates_here[j] + tn(
            terms, ordered, precision=HIGHEST
        )


def scatter_kernel(peers, b_ref, c_ref, gb_ref, gc_ref, near, summed, far, sems):
    seq, me = lax.axis_index("seq"), lax.axis_index("head")
    rows = gb_ref.shape[0]
    rows_of = lambda q: pl.ds(pl.multiple_of(q * rows, rows), rows)
    chips = peers // 2
    core, chip = lax.rem(me, 2), me // 2
    other = me + 1 - 2 * core
    barrier = pltpu.get_barrier_semaphore()
    pl.semaphore_signal(barrier, inc=1, device_id=(seq, other), device_id_type=MESH)
    for k in range(1, chips):
        to = lax.rem(chip + k, chips) * 2 + core
        pl.semaphore_signal(barrier, inc=1, device_id=(seq, to), device_id_type=MESH)
    pl.semaphore_wait(barrier, chips)

    refs = (b_ref, c_ref)
    copies = []
    for k in list(range(1, chips)) + [0]:
        at = lax.rem(chip + k, chips)
        for m in range(2):
            copy = pltpu.make_async_remote_copy(
                src_ref=refs[m].at[rows_of(at * 2 + 1 - core)],
                dst_ref=near.at[k, m],
                send_sem=sems.at[0, k, m], recv_sem=sems.at[1, k, m],
                device_id=(seq, other), device_id_type=MESH,
            )
            copy.start()
            copies.append((k, m, at, copy))
    sent = []
    for k, m, at, copy in copies:
        copy.wait_recv()
        summed[k, m] = refs[m][rows_of(at * 2 + core), :] + near[k, m]
        if k:
            onward = pltpu.make_async_remote_copy(
                src_ref=summed.at[k, m], dst_ref=far.at[k, m],
                send_sem=sems.at[2, k, m], recv_sem=sems.at[3, k, m],
                device_id=(seq, at * 2 + core), device_id_type=MESH,
            )
            onward.start()
            sent.append((k, m, onward))
    totals = [summed[0, m] for m in range(2)]
    for k, m, onward in sent:
        onward.wait_recv()
        totals[m] = totals[m] + far[k, m]
    gb_ref[...] = totals[0]
    gc_ref[...] = totals[1]
    for _, _, _, copy in copies:
        copy.wait_send()
    for _, _, onward in sent:
        onward.wait_send()


def on_device(peers, head_peers, inputs, in_map, out_map, log_decay, cotangent):
    heads, tokens = log_decay.shape
    width = inputs.shape[1] // heads
    states = in_map.shape[1]
    groups = heads // GROUP
    columns = GROUP * width
    chunks = tokens // CHUNK
    rates = log_decay.reshape(groups, GROUP, chunks, CHUNK).transpose(0, 2, 1, 3)
    rates = rates.reshape(groups, chunks * GROUP, CHUNK)
    vmem = pl.BlockSpec(memory_space=pltpu.VMEM)
    channel_block = pl.BlockSpec((tokens, columns), lambda i: (0, i))
    map_block = pl.BlockSpec((tokens, states), lambda i: (0, 0))
    rate_block = pl.BlockSpec((1, chunks * GROUP, CHUNK), lambda i: (i, 0, 0))
    state_block = pl.BlockSpec((GROUP, states, width), lambda i: (i, 0, 0))
    state_shape = jax.ShapeDtypeStruct((heads, states, width), F32)
    channel_shape = jax.ShapeDtypeStruct(inputs.shape, F32)
    map_shape = jax.ShapeDtypeStruct((tokens, states), F32)
    params = pltpu.CompilerParams(
        dimension_semantics=("arbitrary",), vmem_limit_bytes=VMEM_BYTES
    )
    s_here, e_here, totals = pl.pallas_call(
        states_kernel,
        grid=(groups,),
        in_specs=[channel_block, map_block, map_block, rate_block, channel_block],
        out_specs=[state_block, state_block, pl.BlockSpec((GROUP, 8, width), lambda i: (i, 0, 0))],
        out_shape=[state_shape, state_shape, jax.ShapeDtypeStruct((heads, 8, width), F32)],
        compiler_params=params,
        name="shard_states",
    )(inputs, in_map, out_map, rates, cotangent)

    items = heads * SPLIT
    message = (items, states // SPLIT, width)
    message_shape = jax.ShapeDtypeStruct(message, F32)
    s_in, e_in, grad_inputs, grad_in, grad_out, grad_rates = pl.pallas_call(
        functools.partial(chain_kernel, peers, groups),
        in_specs=[vmem] * 8,
        out_specs=[vmem] * 6,
        out_shape=[
            message_shape, message_shape, channel_shape, map_shape, map_shape,
            jax.ShapeDtypeStruct((groups * chunks, GROUP, CHUNK), F32),
        ],
        scratch_shapes=[
            pltpu.VMEM(message, F32),
            pltpu.VMEM(message, F32),
            pltpu.SemaphoreType.DMA((items,)),
            pltpu.SemaphoreType.DMA((items,)),
            pltpu.SemaphoreType.DMA((items,)),
            pltpu.SemaphoreType.DMA((items,)),
            pltpu.VMEM((chunks, CHUNK, GROUP), F32),
            pltpu.VMEM((chunks, CHUNK, GROUP), F32),
            pltpu.VMEM((chunks, 8, columns), F32),
            pltpu.VMEM((chunks, 4, CHUNK, CHUNK), BF16),
            pltpu.VMEM((chunks + 1, states, columns), F32),
            pltpu.VMEM((tokens, columns), BF16),
            pltpu.VMEM((tokens, columns), BF16),
            pltpu.VMEM((states, columns), F32),
            pltpu.VMEM((chunks, CHUNK, CHUNK), F32),
        ],
        compiler_params=pltpu.CompilerParams(
            collective_id=0, has_side_effects=True, vmem_limit_bytes=VMEM_BYTES
        ),
        name="carry_chain",
    )(
        s_here.reshape(message), e_here.reshape(message), totals,
        inputs, in_map, out_map, rates, cotangent,
    )
    s_in = s_in.reshape(heads, states, width)
    e_in = e_in.reshape(heads, states, width)

    grad_inputs, grad_in, grad_out, grad_rates = pl.pallas_call(
        carried_kernel,
        grid=(groups,),
        in_specs=[
            channel_block, map_block, map_block, rate_block, channel_block, state_block, state_block,
            channel_block, map_block, map_block,
            pl.BlockSpec((chunks, GROUP, CHUNK), lambda i: (i, 0, 0)),
        ],
        out_specs=[
            channel_block, map_block, map_block,
            pl.BlockSpec((1, GROUP, tokens), lambda i: (i, 0, 0)),
        ],
        out_shape=[
            channel_shape, map_shape, map_shape, jax.ShapeDtypeStruct((groups, GROUP, tokens), F32)
        ],
        compiler_params=params,
        name="carried_gradients",
    )(
        inputs, in_map, out_map, rates, cotangent, s_in, e_in,
        grad_inputs, grad_in, grad_out, grad_rates,
    )

    rows = tokens // head_peers
    chips = head_peers // 2
    piece = jax.ShapeDtypeStruct((rows, states), F32)
    grad_in, grad_out = pl.pallas_call(
        functools.partial(scatter_kernel, head_peers),
        in_specs=[vmem, vmem],
        out_specs=[vmem, vmem],
        out_shape=[piece, piece],
        scratch_shapes=[
            pltpu.VMEM((chips, 2, rows, states), F32),
            pltpu.VMEM((chips, 2, rows, states), F32),
            pltpu.VMEM((chips, 2, rows, states), F32),
            pltpu.SemaphoreType.DMA((4, chips, 2)),
        ],
        compiler_params=pltpu.CompilerParams(
            collective_id=1, has_side_effects=True, vmem_limit_bytes=VMEM_BYTES
        ),
        name="map_scatter",
    )(grad_in, grad_out)
    return grad_inputs, grad_in, grad_out, grad_rates.reshape(heads, tokens)


def solution(mesh):
    placed = (P("seq", "head"), P("seq", None), P("seq", None), P("head", "seq"), P("seq", "head"))
    return jax.shard_map(
        functools.partial(on_device, mesh.shape["seq"], mesh.shape["head"]),
        mesh=mesh,
        in_specs=placed,
        out_specs=(
            P("seq", "head"),
            P(("seq", "head"), None),
            P(("seq", "head"), None),
            P("head", "seq"),
        ),
        check_vma=False,
    )
```

time: 214 us -> 156 us (0.73)
  waiting for transfers between devices: 44.5 us -> 0 us
  between operations: 14 us -> 0.66 us
  local copies, waits for them, and re-layouts: 2.98 us -> 6.13 us
  Pallas kernels: 152 us -> 149 us
    reduce_scatter x2 -> x0, waiting for transfers between devices: 43.8 us -> none  [on_device(): lax.psum_scatter(g, 'head', scatter_dimension=0, tiled=True)]
    pallas_call x1, Pallas kernels: 19.7 us -> 11.5 us  [on_device(): pl.pallas_call(states_kernel, grid=(groups,), in_specs=[channel_block, ma...]
    pallas_call x2 -> x3, Pallas kernels: 133 us -> 138 us  [the longest x1 97.9 us: on_device(): pl.pallas_call(functools.partial(chain_kernel, peers, groups), in_specs=[...]
    unnamed x0 -> x3, local copies, waits for them, and re-layouts: none -> 3.99 us
  transfers between devices with their start and end apart: 2 -> 0, of which waited for: 2 -> 0; matrix products, arithmetic and copies ran while one was open for 1% -> 0% of each run, Pallas kernels for 0% -> 0%
where the time goes in v2:
time: 156 us
  Pallas kernels  149 us (96%)
  local copies, waits for them, and re-layouts  6.13 us (4%)
    pallas_call x1, Pallas kernels, on_device(): pl.pallas_call(functools.partial(chain_kernel, peers, groups), in_specs=[...  97.9 us
    pallas_call x1, Pallas kernels, on_device(): pl.pallas_call(carried_kernel, grid=(groups,), in_specs=[channel_block, m...  28 us
    pallas_call x1, Pallas kernels, on_device(): pl.pallas_call(functools.partial(scatter_kernel, head_peers), in_specs=[v...  11.9 us
    pallas_call x1, Pallas kernels, on_device(): pl.pallas_call(states_kernel, grid=(groups,), in_specs=[channel_block, ma...  11.5 us
    unnamed x3, local copies, waits for them, and re-layouts  3.99 us

profile of v2, /device:TPU:0, one launch (start us, length us, event | category | flops | bytes accessed | tf_op | source)
XLA Modules:
  0.0 156.1 jit_solution(17099528449299763173)
XLA Ops:
  0.6 0.9 copy.10
  1.5 0.6 copy.9
  2.1 11.5 %shard_states.1 = (f32[16,128,128]{2,1,0:T(8,128)}, f32[16,128,128]{2,1,0:T(8,128)}, f32[16,8,128]{2,1,0:T(8,128)}) custom-call(bf16[1024,2048]{1,0:T(8,128)(2,1)} %x_ref.5, bf16[1024,128]{1,0:T(8,128)(2,1)} %b_ref.5, bf16[1024,128]{1,0:T(8,128)(2,1)} %c_ref.5, f32[4,32,128]{2,1,0:T(8,128)} %bitcast.10, bf16[1024,2048]{1,0:T(8,128)(2,1)} %dy_ref.5), custom_call_target="tpu_custom_call" | custom-call | tf_op jit(solution)/shard_map/shard_states/pallas_call | solution.py:449
  13.6 97.9 %carry_chain.1 = (f32[32,64,128]{2,1,0:T(8,128)}, f32[32,64,128]{2,1,0:T(8,128)}, f32[1024,2048]{1,0:T(8,128)}, f32[1024,128]{1,0:T(8,128)}, f32[1024,128]{1,0:T(8,128)}, /*index=5*/f32[32,4,128]{2,1,0:T(4,128)}) custom-call(f32[32,64,128]{2,1,0:T(8,128)} %bitcast.15, f32[32,64,128]{2,1,0:T(8,128)} %bitcast.16, f32[16,8,128]{2,1,0:T(8,128)} %get-tuple-element.21.total_ref, ...), custom_call_target="tpu_custom_call" | custom-call | tf_op jit(solution)/shard_map/carry_chain/pallas_call | solution.py:462
  111.5 28.0 %carried_gradients.1 = (f32[1024,2048]{1,0:T(8,128)}, f32[1024,128]{1,0:T(8,128)}, f32[1024,128]{1,0:T(8,128)}, f32[4,4,1024]{2,1,0:T(4,128)}) custom-call(bf16[1024,2048]{1,0:T(8,128)(2,1)} %x_ref.5, bf16[1024,128]{1,0:T(8,128)(2,1)} %b_ref.5, bf16[1024,128]{1,0:T(8,128)(2,1)} %c_ref.5, f32[4,32,128]{2,1,0:T(8,128)} %bitcast.12, bf16[1024,2048]{1,0:T(8,128)(2,1)} %dy_ref.5, ...), custom_call_target="tpu_custom_call" | custom-call | tf_op jit(solution)/shard_map/carried_gradients/pallas_call | solution.py:498
  139.6 1.5 reshape.35
  141.1 11.9 %map_scatter.1 = (f32[256,128]{1,0:T(8,128)}, f32[256,128]{1,0:T(8,128)}) custom-call(f32[1024,128]{1,0:T(8,128)} %get-tuple-element.29.b_ref, f32[1024,128]{1,0:T(8,128)} %get-tuple-element.30.c_ref), custom_call_target="tpu_custom_call" | custom-call | tf_op jit(solution)/shard_map/map_scatter/pallas_call | solution.py:523
  153.0 1.6 %copy.13 = f32[256,128]{1,0:T(8,128)} copy(f32[256,128]{1,0:T(8,128)} %get-tuple-element.39) | data formatting | bytes 262144
  154.6 1.6 %copy.14 = f32[256,128]{1,0:T(8,128)} copy(f32[256,128]{1,0:T(8,128)} %get-tuple-element.40) | data formatting | bytes 262144

commit v3 on v2

--- a/solution.py
+++ b/solution.py
@@ -165,7 +165,6 @@
     pairs = chunks // 2
     period = chunks + pairs
     causal = order()
-    after = jnp.logical_not(causal).astype(F32)
 
     gb_ref[...] = jnp.zeros_like(gb_ref)
     gc_ref[...] = jnp.zeros_like(gc_ref)
@@ -225,11 +224,8 @@
         )
         gx_ref[rows, cols] = g_wide * z
         fy = fy_hi.astype(F32) + fy_lo.astype(F32)
-        turnover = per_head(gx * z - fy * y, heads)
-        crossing = per_head(adjoints[j] * state, heads)
-        rates_out[group * chunks + j] = tn(turnover, after, precision=HIGHEST) + tn(
-            crossing, jnp.ones((states, CHUNK), F32), precision=HIGHEST
-        )
+        turnover = jnp.concatenate([gx * z - fy * y, adjoints[j] * state], axis=1)
+        rates_out[group * chunks + j] = per_head(turnover, 2 * heads)
         both = nt(
             jnp.concatenate([fy_hi, fy_hi, fy_lo], axis=1),
             jnp.concatenate(
@@ -337,42 +333,54 @@
     s_all = [s_ref[h] for h in range(heads)]
     e_all = [e_ref[h] for h in range(heads)]
     crossing = per_head(jnp.concatenate([s * e for s, e in zip(s_all, e_all)], axis=1), heads) * total
-    s_parts = [jnp.concatenate(split(s), axis=1) for s in s_all]
-    e_parts = [jnp.concatenate(split(e), axis=1) for e in e_all]
-    e_rows = jnp.concatenate(split(jnp.concatenate(e_all, axis=1)), axis=0)
     lane = lax.broadcasted_iota(jnp.int32, (CHUNK, heads), 1)
-    outs, ins = [], []
+    outs = [jnp.zeros((CHUNK, heads), F32)] * chunks
+    ins = [rates_here[j][:, :heads] for j in range(chunks)]
+    b, c = b_ref[...], c_ref[...]
+    b_twice = jnp.concatenate([b, b], axis=1)
+    for h in range(heads):
+        here = slice(h * width, (h + 1) * width)
+        x, dy = x_ref[:, here], dy_ref[:, here]
+        e_parts = split(e_all[h])
+        z = nn(b_twice, jnp.concatenate(e_parts, axis=0))
+        feed_out = nt(
+            jnp.concatenate([dy, dy], axis=1), jnp.concatenate(split(s_all[h]), axis=1)
+        )
+        feed_in = nt(jnp.concatenate([x, x], axis=1), jnp.concatenate(e_parts, axis=1))
+        for j in range(chunks):
+            rows = slice(j * CHUNK, (j + 1) * CHUNK)
+            col = j * heads + h
+            fs = jnp.broadcast_to(from_start[:, col : col + 1], (CHUNK, width))
+            te = jnp.broadcast_to(to_end[:, col : col + 1], (CHUNK, width))
+            gx_ref[rows, here] = gx_here[rows, here] + te * z[rows, :]
+            out, back = fs * feed_out[rows, :], te * feed_in[rows, :]
+            gc_ref[rows, :] += out
+            gb_ref[rows, :] += back
+            out_sum = jnp.sum(out * c[rows, :].astype(F32), axis=1, keepdims=True)
+            in_sum = jnp.sum(back * b[rows, :].astype(F32), axis=1, keepdims=True)
+            outs[j] = jnp.where(lane == h, out_sum, outs[j])
+            ins[j] = jnp.where(lane == h, ins[j] + in_sum, ins[j])
+    beyond = []
     for j in range(chunks):
-        rows = pl.ds(j * CHUNK, CHUNK)
-        at = slice(j * heads, (j + 1) * heads)
-        fs, te = from_start[:, at], to_end[:, at]
-        b, c = b_ref[rows, :], c_ref[rows, :]
-        b_wide, c_wide = b.astype(F32), c.astype(F32)
-        z = nn(jnp.concatenate([b, b], axis=1), e_rows)
-        gb, gc = gb_ref[rows, :], gc_ref[rows, :]
-        d_out = d_in = jnp.zeros((CHUNK, heads), F32)
-        for h in range(heads):
-            here = slice(h * width, (h + 1) * width)
-            x, dy = x_ref[rows, here], dy_ref[rows, here]
-            fs_h = jnp.broadcast_to(fs[:, h : h + 1], (CHUNK, width))
-            te_h = jnp.broadcast_to(te[:, h : h + 1], (CHUNK, width))
-            gx_ref[rows, here] = gx_here[rows, here] + te_h * z[:, here]
-            feed_out = fs_h * nt(jnp.concatenate([dy, dy], axis=1), s_parts[h])
-            feed_in = te_h * nt(jnp.concatenate([x, x], axis=1), e_parts[h])
-            gc += feed_out
-            gb += feed_in
-            d_out = jnp.where(lane == h, jnp.sum(feed_out * c_wide, axis=1, keepdims=True), d_out)
-            d_in = jnp.where(lane == h, jnp.sum(feed_in * b_wide, axis=1, keepdims=True), d_in)
-        gb_ref[rows, :] = gb
-        gc_ref[rows, :] = gc
-        outs.append(d_out)
-        ins.append(d_in)
-    for j in range(chunks):
-        beyond = crossing + sum(outs[j + 1 :]) + sum(ins[:j])
-        terms = jnp.concatenate([outs[j], ins[j], beyond], axis=0)
-        rates_out[0, :, pl.ds(j * CHUNK, CHUNK)] = rates_here[j] + tn(
-            terms, ordered, precision=HIGHEST
-        )
+        others = crossing + rates_here[j][:, heads:]
+        for k in range(chunks):
+            if k > j:
+                others = others + outs[k]
+            elif k < j:
+                others = others + (ins[k] - rates_here[k][:, :heads])
+        beyond.append(others)
+    terms = jnp.concatenate(
+        [jnp.concatenate(part, axis=1) for part in (outs, ins, beyond)], axis=0
+    )
+    sums = tn(terms, ordered, precision=HIGHEST)
+    for k in range(rates_out.shape[0] // heads):
+
+        @pl.when(pl.program_id(0) == k)
+        def _():
+            for j in range(chunks):
+                rates_out[pl.ds(k * heads, heads), pl.ds(j * CHUNK, CHUNK)] = sums[
+                    j * heads : (j + 1) * heads, :
+                ]
 
 
 def scatter_kernel(peers, b_ref, c_ref, gb_ref, gc_ref, near, summed, far, sems):
@@ -465,7 +473,7 @@
         out_specs=[vmem] * 6,
         out_shape=[
             message_shape, message_shape, channel_shape, map_shape, map_shape,
-            jax.ShapeDtypeStruct((groups * chunks, GROUP, CHUNK), F32),
+            jax.ShapeDtypeStruct((groups * chunks, CHUNK, 2 * GROUP), F32),
         ],
         scratch_shapes=[
             pltpu.VMEM(message, F32),
@@ -501,14 +509,14 @@
         in_specs=[
             channel_block, map_block, map_block, rate_block, channel_block, state_block, state_block,
             channel_block, map_block, map_block,
-            pl.BlockSpec((chunks, GROUP, CHUNK), lambda i: (i, 0, 0)),
+            pl.BlockSpec((chunks, CHUNK, 2 * GROUP), lambda i: (i, 0, 0)),
         ],
         out_specs=[
             channel_block, map_block, map_block,
-            pl.BlockSpec((1, GROUP, tokens), lambda i: (i, 0, 0)),
+            pl.BlockSpec((heads, tokens), lambda i: (0, 0)),
         ],
         out_shape=[
-            channel_shape, map_shape, map_shape, jax.ShapeDtypeStruct((groups, GROUP, tokens), F32)
+            channel_shape, map_shape, map_shape, jax.ShapeDtypeStruct((heads, tokens), F32)
         ],
         compiler_params=params,
         name="carried_gradients",
@@ -536,7 +544,7 @@
         ),
         name="map_scatter",
     )(grad_in, grad_out)
-    return grad_inputs, grad_in, grad_out, grad_rates.reshape(heads, tokens)
+    return grad_inputs, grad_in, grad_out, grad_rates
 
 
 def solution(mesh):

time: 156 us -> 156 us (level)
  Pallas kernels: 149 us -> 151 us
    pallas_call x1, Pallas kernels: 28 us -> 30.5 us  [on_device(): pl.pallas_call(carried_kernel, grid=(groups,), in_specs=[channel_block, m...]
where the time goes in v3:
time: 156 us
  Pallas kernels  151 us (97%)
  local copies, waits for them, and re-layouts  4.64 us (3%)
    pallas_call x1, Pallas kernels, on_device(): pl.pallas_call(functools.partial(chain_kernel, peers, groups), in_specs=[...  96.5 us
    pallas_call x1, Pallas kernels, on_device(): pl.pallas_call(carried_kernel, grid=(groups,), in_specs=[channel_block, m...  30.5 us
    pallas_call x1, Pallas kernels, on_device(): pl.pallas_call(functools.partial(scatter_kernel, head_peers), in_specs=[v...  11.9 us
    pallas_call x1, Pallas kernels, on_device(): pl.pallas_call(states_kernel, grid=(groups,), in_specs=[channel_block, ma...  11.5 us
    unnamed x3, local copies, waits for them, and re-layouts  3.99 us

profile of v3, /device:TPU:0, one launch (start us, length us, event | category | flops | bytes accessed | tf_op | source)
XLA Modules:
  0.0 155.8 jit_solution(7380518160888767422)
XLA Ops:
  0.6 0.9 copy.10
  1.5 0.6 copy.9
  2.1 11.5 %shard_states.1 = (f32[16,128,128]{2,1,0:T(8,128)}, f32[16,128,128]{2,1,0:T(8,128)}, f32[16,8,128]{2,1,0:T(8,128)}) custom-call(bf16[1024,2048]{1,0:T(8,128)(2,1)} %x_ref.5, bf16[1024,128]{1,0:T(8,128)(2,1)} %b_ref.5, bf16[1024,128]{1,0:T(8,128)(2,1)} %c_ref.5, f32[4,32,128]{2,1,0:T(8,128)} %bitcast.10, bf16[1024,2048]{1,0:T(8,128)(2,1)} %dy_ref.5), custom_call_target="tpu_custom_call" | custom-call | tf_op jit(solution)/shard_map/shard_states/pallas_call | solution.py:457
  13.7 96.5 %carry_chain.1 = (f32[32,64,128]{2,1,0:T(8,128)}, f32[32,64,128]{2,1,0:T(8,128)}, f32[1024,2048]{1,0:T(8,128)}, f32[1024,128]{1,0:T(8,128)}, f32[1024,128]{1,0:T(8,128)}, /*index=5*/f32[32,128,8]{2,1,0:T(8,128)}) custom-call(f32[32,64,128]{2,1,0:T(8,128)} %bitcast.15, f32[32,64,128]{2,1,0:T(8,128)} %bitcast.16, f32[16,8,128]{2,1,0:T(8,128)} %get-tuple-element.21.total_ref, ...), custom_call_target="tpu_custom_call" | custom-call | tf_op jit(solution)/shard_map/carry_chain/pallas_call | solution.py:470
  110.2 30.5 %carried_gradients.1 = (f32[1024,2048]{1,0:T(8,128)}, f32[1024,128]{1,0:T(8,128)}, f32[1024,128]{1,0:T(8,128)}, f32[16,1024]{1,0:T(8,128)}) custom-call(bf16[1024,2048]{1,0:T(8,128)(2,1)} %x_ref.5, bf16[1024,128]{1,0:T(8,128)(2,1)} %b_ref.5, bf16[1024,128]{1,0:T(8,128)(2,1)} %c_ref.5, f32[4,32,128]{2,1,0:T(8,128)} %bitcast.12, bf16[1024,2048]{1,0:T(8,128)(2,1)} %dy_ref.5, ...), custom_call_target="tpu_custom_call" | custom-call | tf_op jit(solution)/shard_map/carried_gradients/pallas_call | solution.py:506
  140.7 11.9 %map_scatter.1 = (f32[256,128]{1,0:T(8,128)}, f32[256,128]{1,0:T(8,128)}) custom-call(f32[1024,128]{1,0:T(8,128)} %get-tuple-element.29.b_ref, f32[1024,128]{1,0:T(8,128)} %get-tuple-element.30.c_ref), custom_call_target="tpu_custom_call" | custom-call | tf_op jit(solution)/shard_map/map_scatter/pallas_call | solution.py:531
  152.7 1.6 %copy.13 = f32[256,128]{1,0:T(8,128)} copy(f32[256,128]{1,0:T(8,128)} %get-tuple-element.39) | data formatting | bytes 262144
  154.3 1.6 %copy.14 = f32[256,128]{1,0:T(8,128)} copy(f32[256,128]{1,0:T(8,128)} %get-tuple-element.40) | data formatting | bytes 262144

commit v4 on v3

--- a/solution.py
+++ b/solution.py
@@ -58,6 +58,32 @@
     for h, part in enumerate(heads_of(v, v.shape[1] // heads)):
         out = jnp.where(lane == h, jnp.sum(part, axis=1, keepdims=True), out)
     return out
+
+
+def columns_of(v):
+    hi = v.astype(BF16).astype(F32)
+    mid = (v - hi).astype(BF16).astype(F32)
+    return jnp.concatenate([hi, mid, v - hi - mid], axis=0).T.astype(BF16)
+
+
+def fill_spread(spread_ref, heads, width):
+    chunks, depth, columns = spread_ref.shape
+    row = lax.rem(lax.broadcasted_iota(jnp.int32, (depth, columns), 0), depth // 3)
+    head = lax.div(lax.broadcasted_iota(jnp.int32, (depth, columns), 1), width)
+    for j in range(chunks):
+        spread_ref[j] = (row == head + j * heads).astype(F32).astype(BF16)
+
+
+def fill_gather(gather_ref, width):
+    shape = gather_ref.shape
+    row = lax.div(lax.broadcasted_iota(jnp.int32, shape, 0), width)
+    gather_ref[...] = (row == lax.broadcasted_iota(jnp.int32, shape, 1)).astype(F32).astype(BF16)
+
+
+def head_sums(v, gather_ref):
+    hi, lo = split(v)
+    sums = gather_ref[...]
+    return nn(hi, sums) + nn(lo, sums)
 
 
 def running_of(rates):
@@ -78,22 +104,27 @@
     wide_last = jnp.broadcast_to(last, run.shape)
     earlier = nn(jnp.logical_and(same, col < row).astype(F32), wide_last, precision=HIGHEST)
     later = nn(jnp.logical_and(same, col > row).astype(F32), wide_last, precision=HIGHEST)
-    from_start = (jnp.exp(earlier) * jnp.exp(run)).T
-    to_end = jnp.exp(later + (last - run)).T
-    return from_start, to_end, from_start[CHUNK - 1 : CHUNK, rows - heads :]
-
-
-def states_kernel(x_ref, b_ref, c_ref, rate_ref, dy_ref, s_ref, e_ref, total_ref):
+    from_start = jnp.exp(earlier) * jnp.exp(run)
+    to_end = jnp.exp(later + (last - run))
+    total = from_start.T[CHUNK - 1 : CHUNK, rows - heads :]
+    return columns_of(from_start), columns_of(to_end), total
+
+
+def states_kernel(x_ref, b_ref, c_ref, rate_ref, dy_ref, s_ref, e_ref, total_ref, spread_ref):
     tokens, columns = x_ref.shape
     heads, width = s_ref.shape[0], s_ref.shape[2]
+
+    @pl.when(pl.program_id(0) == 0)
+    def _():
+        fill_spread(spread_ref, heads, width)
+
     from_start, to_end, total = shard_decays(rate_ref[0], heads)
 
     def scaled(ref, factors):
         parts = []
         for j in range(tokens // CHUNK):
             rows = pl.ds(j * CHUNK, CHUNK)
-            cols = factors[:, j * heads : (j + 1) * heads]
-            parts.append(split(wide(cols, width) * ref[rows, :].astype(F32)))
+            parts.append(split(nn(factors, spread_ref[j]) * ref[rows, :].astype(F32)))
         return jnp.concatenate([hi for hi, _ in parts] + [lo for _, lo in parts], axis=0)
 
     def twice(ref):
@@ -112,7 +143,7 @@
     peers, groups, s_ref, e_ref, total_ref, x_ref, b_ref, c_ref, rate_ref, dy_ref,
     s_in, e_in, gx_ref, gb_ref, gc_ref, rates_out,
     s_out, e_out, s_send, s_recv, e_send, e_recv,
-    f_ref, g_ref, end_ref, scores_ref, adjoints, fy_hi_ref, fy_lo_ref, state_ref, joint,
+    f_ref, g_ref, end_ref, spread_ref, gather_ref, scores_ref, adjoints, fy_hi_ref, fy_lo_ref, state_ref, joint,
 ):
     me, lane = lax.axis_index("seq"), lax.axis_index("head")
     items = s_ref.shape[0]
@@ -166,6 +197,8 @@
     period = chunks + pairs
     causal = order()
 
+    fill_spread(spread_ref, heads, width)
+    fill_gather(gather_ref, width)
     gb_ref[...] = jnp.zeros_like(gb_ref)
     gc_ref[...] = jnp.zeros_like(gc_ref)
     joint[...] = jnp.zeros_like(joint)
@@ -174,12 +207,12 @@
         run = running_of(rate_ref[group])
         mid = run[:, CHUNK // 2 - 1 : CHUNK // 2]
         f = jnp.exp(run - mid)
-        f_cols, g_cols = f.T, jnp.exp(mid - run).T
+        f_cols = f.T
+        f_ref[...] = columns_of(f)
+        g_ref[...] = columns_of(jnp.exp(mid - run))
         m_cols = jnp.broadcast_to(jnp.exp(mid), run.shape).T
         for j in range(chunks):
             at = slice(j * heads, (j + 1) * heads)
-            f_ref[j] = f_cols[:, at]
-            g_ref[j] = g_cols[:, at]
             end_ref[j, 0:1, :] = wide(m_cols[0:1, at], width)
             end_ref[j, 1:2, :] = wide(f_cols[CHUNK - 1 : CHUNK, at], width)
 
@@ -194,7 +227,7 @@
         rows = pl.ds(pl.multiple_of(j * CHUNK, CHUNK), CHUNK)
         cols = pl.ds(pl.multiple_of(group * columns, columns), columns)
         mid, last = end_ref[j, 0:1, :], end_ref[j, 1:2, :]
-        fy_hi, fy_lo = split(wide(f_ref[j], width) * dy_ref[rows, cols].astype(F32))
+        fy_hi, fy_lo = split(nn(f_ref[...], spread_ref[j]) * dy_ref[rows, cols].astype(F32))
         fy_hi_ref[rows, :] = fy_hi
         fy_lo_ref[rows, :] = fy_lo
         c = c_ref[rows, :].T
@@ -205,7 +238,7 @@
         rows = pl.ds(pl.multiple_of(j * CHUNK, CHUNK), CHUNK)
         cols = pl.ds(pl.multiple_of(group * columns, columns), columns)
         mid, last = end_ref[j, 0:1, :], end_ref[j, 1:2, :]
-        g_wide = wide(g_ref[j], width)
+        g_wide = nn(g_ref[...], spread_ref[j])
         b, c = b_ref[rows, :], c_ref[rows, :]
         gx = g_wide * x_ref[rows, cols].astype(F32)
         gx_hi, gx_lo = split(gx)
@@ -225,7 +258,7 @@
         gx_ref[rows, cols] = g_wide * z
         fy = fy_hi.astype(F32) + fy_lo.astype(F32)
         turnover = jnp.concatenate([gx * z - fy * y, adjoints[j] * state], axis=1)
-        rates_out[group * chunks + j] = per_head(turnover, 2 * heads)
+        rates_out[group * chunks + j] = head_sums(turnover, gather_ref)
         both = nt(
             jnp.concatenate([fy_hi, fy_hi, fy_lo], axis=1),
             jnp.concatenate(
@@ -313,7 +346,7 @@
 
 def carried_kernel(
     x_ref, b_ref, c_ref, rate_ref, dy_ref, s_ref, e_ref, gx_here, gb_here, gc_here, rates_here,
-    gx_ref, gb_ref, gc_ref, rates_out,
+    gx_ref, gb_ref, gc_ref, rates_out, spread_ref, gather_ref,
 ):
     tokens, columns = x_ref.shape
     heads, states, width = s_ref.shape
@@ -327,39 +360,40 @@
 
     @pl.when(pl.program_id(0) == 0)
     def _():
+        fill_spread(spread_ref, heads, width)
+        fill_gather(gather_ref, width)
         gb_ref[...] = gb_here[...]
         gc_ref[...] = gc_here[...]
 
     s_all = [s_ref[h] for h in range(heads)]
     e_all = [e_ref[h] for h in range(heads)]
     crossing = per_head(jnp.concatenate([s * e for s, e in zip(s_all, e_all)], axis=1), heads) * total
-    lane = lax.broadcasted_iota(jnp.int32, (CHUNK, heads), 1)
-    outs = [jnp.zeros((CHUNK, heads), F32)] * chunks
-    ins = [rates_here[j][:, :heads] for j in range(chunks)]
-    b, c = b_ref[...], c_ref[...]
-    b_twice = jnp.concatenate([b, b], axis=1)
-    for h in range(heads):
-        here = slice(h * width, (h + 1) * width)
-        x, dy = x_ref[:, here], dy_ref[:, here]
-        e_parts = split(e_all[h])
-        z = nn(b_twice, jnp.concatenate(e_parts, axis=0))
-        feed_out = nt(
-            jnp.concatenate([dy, dy], axis=1), jnp.concatenate(split(s_all[h]), axis=1)
-        )
-        feed_in = nt(jnp.concatenate([x, x], axis=1), jnp.concatenate(e_parts, axis=1))
-        for j in range(chunks):
-            rows = slice(j * CHUNK, (j + 1) * CHUNK)
-            col = j * heads + h
-            fs = jnp.broadcast_to(from_start[:, col : col + 1], (CHUNK, width))
-            te = jnp.broadcast_to(to_end[:, col : col + 1], (CHUNK, width))
-            gx_ref[rows, here] = gx_here[rows, here] + te * z[rows, :]
-            out, back = fs * feed_out[rows, :], te * feed_in[rows, :]
-            gc_ref[rows, :] += out
-            gb_ref[rows, :] += back
-            out_sum = jnp.sum(out * c[rows, :].astype(F32), axis=1, keepdims=True)
-            in_sum = jnp.sum(back * b[rows, :].astype(F32), axis=1, keepdims=True)
-            outs[j] = jnp.where(lane == h, out_sum, outs[j])
-            ins[j] = jnp.where(lane == h, ins[j] + in_sum, ins[j])
+    s_parts = [jnp.concatenate(split(s), axis=1) for s in s_all]
+    e_parts = [jnp.concatenate(split(e), axis=1) for e in e_all]
+    e_rows = jnp.concatenate(split(jnp.concatenate(e_all, axis=1)), axis=0)
+
+    def feed(ref, rows, parts):
+        out = []
+        for h in range(heads):
+            v = ref[rows, pl.ds(h * width, width)]
+            out.append(nt(jnp.concatenate([v, v], axis=1), parts[h]))
+        return jnp.concatenate(out, axis=1)
+
+    outs, carried, ins = [], [], []
+    for j in range(chunks):
+        rows = pl.ds(j * CHUNK, CHUNK)
+        b, c = b_ref[rows, :], c_ref[rows, :]
+        fs, te = nn(from_start, spread_ref[j]), nn(to_end, spread_ref[j])
+        gx_ref[rows, :] = gx_here[rows, :] + te * nn(jnp.concatenate([b, b], axis=1), e_rows)
+        out, back = fs * feed(dy_ref, rows, s_parts), te * feed(x_ref, rows, e_parts)
+        gc_ref[rows, :] += sum(heads_of(out, width))
+        gb_ref[rows, :] += sum(heads_of(back, width))
+        b_wide = jnp.concatenate([b.astype(F32)] * heads, axis=1)
+        c_wide = jnp.concatenate([c.astype(F32)] * heads, axis=1)
+        both = head_sums(jnp.concatenate([out * c_wide, back * b_wide], axis=1), gather_ref)
+        outs.append(both[:, :heads])
+        carried.append(both[:, heads:])
+        ins.append(both[:, heads:] + rates_here[j][:, :heads])
     beyond = []
     for j in range(chunks):
         others = crossing + rates_here[j][:, heads:]
@@ -367,7 +401,7 @@
             if k > j:
                 others = others + outs[k]
             elif k < j:
-                others = others + (ins[k] - rates_here[k][:, :heads])
+                others = others + carried[k]
         beyond.append(others)
     terms = jnp.concatenate(
         [jnp.concatenate(part, axis=1) for part in (outs, ins, beyond)], axis=0
@@ -454,12 +488,15 @@
     params = pltpu.CompilerParams(
         dimension_semantics=("arbitrary",), vmem_limit_bytes=VMEM_BYTES
     )
+    spread = pltpu.VMEM((chunks, 3 * chunks * GROUP, columns), BF16)
+    gather = pltpu.VMEM((2 * columns, 2 * GROUP), BF16)
     s_here, e_here, totals = pl.pallas_call(
         states_kernel,
         grid=(groups,),
         in_specs=[channel_block, map_block, map_block, rate_block, channel_block],
         out_specs=[state_block, state_block, pl.BlockSpec((GROUP, 8, width), lambda i: (i, 0, 0))],
         out_shape=[state_shape, state_shape, jax.ShapeDtypeStruct((heads, 8, width), F32)],
+        scratch_shapes=[spread],
         compiler_params=params,
         name="shard_states",
     )(inputs, in_map, out_map, rates, cotangent)
@@ -482,9 +519,11 @@
             pltpu.SemaphoreType.DMA((items,)),
             pltpu.SemaphoreType.DMA((items,)),
             pltpu.SemaphoreType.DMA((items,)),
-            pltpu.VMEM((chunks, CHUNK, GROUP), F32),
-            pltpu.VMEM((chunks, CHUNK, GROUP), F32),
+            pltpu.VMEM((CHUNK, 3 * chunks * GROUP), BF16),
+            pltpu.VMEM((CHUNK, 3 * chunks * GROUP), BF16),
             pltpu.VMEM((chunks, 8, columns), F32),
+            spread,
+            gather,
             pltpu.VMEM((chunks, 4, CHUNK, CHUNK), BF16),
             pltpu.VMEM((chunks + 1, states, columns), F32),
             pltpu.VMEM((tokens, columns), BF16),
@@ -518,6 +557,7 @@
         out_shape=[
             channel_shape, map_shape, map_shape, jax.ShapeDtypeStruct((heads, tokens), F32)
         ],
+        scratch_shapes=[spread, gather],
         compiler_params=params,
         name="carried_gradients",
     )(

time: 156 us -> 151 us (0.968)
  Pallas kernels: 151 us -> 146 us
    pallas_call x1, Pallas kernels: 30.5 us -> 24.8 us  [on_device(): pl.pallas_call(carried_kernel, grid=(groups,), in_specs=[channel_block, m...]
where the time goes in v4:
time: 151 us
  Pallas kernels  146 us (97%)
  local copies, waits for them, and re-layouts  4.64 us (3%)
    pallas_call x1, Pallas kernels, on_device(): pl.pallas_call(functools.partial(chain_kernel, peers, groups), in_specs=[...  98.1 us
    pallas_call x1, Pallas kernels, on_device(): pl.pallas_call(carried_kernel, grid=(groups,), in_specs=[channel_block, m...  24.8 us
    pallas_call x1, Pallas kernels, on_device(): pl.pallas_call(functools.partial(scatter_kernel, head_peers), in_specs=[v...  11.9 us
    pallas_call x1, Pallas kernels, on_device(): pl.pallas_call(states_kernel, grid=(groups,), in_specs=[channel_block, ma...  11.1 us
    unnamed x3, local copies, waits for them, and re-layouts  3.99 us

profile of v4, /device:TPU:0, one launch (start us, length us, event | category | flops | bytes accessed | tf_op | source)
XLA Modules:
  0.0 151.2 jit_solution(5937306197623848980)
XLA Ops:
  0.6 0.9 copy.10
  1.5 0.6 copy.9
  2.1 11.1 %shard_states.1 = (f32[16,128,128]{2,1,0:T(8,128)}, f32[16,128,128]{2,1,0:T(8,128)}, f32[16,8,128]{2,1,0:T(8,128)}) custom-call(bf16[1024,2048]{1,0:T(8,128)(2,1)} %x_ref.5, bf16[1024,128]{1,0:T(8,128)(2,1)} %b_ref.5, bf16[1024,128]{1,0:T(8,128)(2,1)} %c_ref.5, f32[4,32,128]{2,1,0:T(8,128)} %bitcast.10, bf16[1024,2048]{1,0:T(8,128)(2,1)} %dy_ref.5), custom_call_target="tpu_custom_call" | custom-call | tf_op jit(solution)/shard_map/shard_states/pallas_call | solution.py:493
  13.2 98.1 %carry_chain.1 = (f32[32,64,128]{2,1,0:T(8,128)}, f32[32,64,128]{2,1,0:T(8,128)}, f32[1024,2048]{1,0:T(8,128)}, f32[1024,128]{1,0:T(8,128)}, f32[1024,128]{1,0:T(8,128)}, /*index=5*/f32[32,128,8]{2,1,0:T(8,128)}) custom-call(f32[32,64,128]{2,1,0:T(8,128)} %bitcast.15, f32[32,64,128]{2,1,0:T(8,128)} %bitcast.16, f32[16,8,128]{2,1,0:T(8,128)} %get-tuple-element.21.total_ref, ...), custom_call_target="tpu_custom_call" | custom-call | tf_op jit(solution)/shard_map/carry_chain/pallas_call | solution.py:507
  111.3 24.8 %carried_gradients.1 = (f32[1024,2048]{1,0:T(8,128)}, f32[1024,128]{1,0:T(8,128)}, f32[1024,128]{1,0:T(8,128)}, f32[16,1024]{1,0:T(8,128)}) custom-call(bf16[1024,2048]{1,0:T(8,128)(2,1)} %x_ref.5, bf16[1024,128]{1,0:T(8,128)(2,1)} %b_ref.5, bf16[1024,128]{1,0:T(8,128)(2,1)} %c_ref.5, f32[4,32,128]{2,1,0:T(8,128)} %bitcast.12, bf16[1024,2048]{1,0:T(8,128)(2,1)} %dy_ref.5, ...), custom_call_target="tpu_custom_call" | custom-call | tf_op jit(solution)/shard_map/carried_gradients/pallas_call | solution.py:545
  136.1 11.9 %map_scatter.1 = (f32[256,128]{1,0:T(8,128)}, f32[256,128]{1,0:T(8,128)}) custom-call(f32[1024,128]{1,0:T(8,128)} %get-tuple-element.29.b_ref, f32[1024,128]{1,0:T(8,128)} %get-tuple-element.30.c_ref), custom_call_target="tpu_custom_call" | custom-call | tf_op jit(solution)/shard_map/map_scatter/pallas_call | solution.py:571
  148.1 1.6 %copy.13 = f32[256,128]{1,0:T(8,128)} copy(f32[256,128]{1,0:T(8,128)} %get-tuple-element.39) | data formatting | bytes 262144
  149.6 1.6 %copy.14 = f32[256,128]{1,0:T(8,128)} copy(f32[256,128]{1,0:T(8,128)} %get-tuple-element.40) | data formatting | bytes 262144
